TPU v7x, 512 devices: a whole 4x4x16 slice. The times are simulated.
512 devices in a mesh: bx: 32 (over x, y, core), by: 16 (over z).
Axes of the slice: x: 4, y: 4, z: 16, core: 2. Of those that a mesh axis runs over, the one named last changes fastest.
Arguments:
- volume: bfloat16 [512, 512, 2048], P('bx', 'by'), may hold values from 0 to 2
- view_side: int32 [512], P('by'), may hold values from 0 to 1
Outputs:
- image: float32 [4, 512, 2048], P(None, 'by', 'bx')
All inputs are finite; a program needn't handle non-finite values.
Results may differ from a plain program's by a relative error of at most 0.0003.
Values may be sent and summed in bfloat16 or wider, within the bound.
No kernel may reach another device: no remote copies, remote signals or barrier semaphores. Data moves between devices by JAX's collectives and lax.ppermute only.
A program may use at most 64 MiB of HBM per device.

v0:
```python
import jax
import jax.numpy as jnp
from jax import lax
from jax.sharding import PartitionSpec as P


def with_halo(x, sides, width):
    for axis, dim in sides:
        size, length = (lax.axis_size(axis), x.shape[dim])
        up = [(i, (i + 1) % size) for i in range(size - 1)]
        down = [(j, i) for i, j in up]
        last = lax.slice_in_dim(x, length - width, length, axis=dim)
        first = lax.slice_in_dim(x, 0, width, axis=dim)
        before = lax.ppermute(last, axis, up)
        after = lax.ppermute(first, axis, down)
        x = jnp.concatenate([before, x, after], axis=dim)
    return x


def shade_block(stencil, ray_length):
    stress = stencil[1:-1, 1:-1, 1:-1]
    grad_x = 0.5 * (stencil[2:, 1:-1, 1:-1] - stencil[:-2, 1:-1, 1:-1])
    grad_y = 0.5 * (stencil[1:-1, 2:, 1:-1] - stencil[1:-1, :-2, 1:-1])
    grad_z = 0.5 * (stencil[1:-1, 1:-1, 2:] - stencil[1:-1, 1:-1, :-2])
    grad_sq = grad_x * grad_x + grad_y * grad_y + grad_z * grad_z
    facing = 0.48 * grad_x + 0.6 * grad_y + 0.64 * grad_z
    shading = 0.3 + 0.7 * facing * facing / (grad_sq + 1.0)
    contour = grad_sq / (grad_sq + 0.25)
    density = jnp.clip((stress - 0.4) / 1.2, 0.0, 1.0)
    opacity = 1.0 - jnp.exp(-3.0 * density * (0.25 + contour) / ray_length)
    weight = opacity * shading
    red_part = jnp.clip(stress - 0.8, 0.0, 1.0)
    green_part = 1.0 - jnp.abs(stress - 1.0)
    blue_part = jnp.clip(1.2 - stress, 0.0, 1.0)
    return jnp.stack([weight * red_part, weight * green_part, weight * blue_part, 1.0 - opacity])


def over(front, back):
    color = front[:3] + front[3:] * back[:3]
    return jnp.concatenate([color, front[3:] * back[3:]], 0)


def fold_layers(stacked):
    while stacked.shape[1] > 1:
        count = stacked.shape[1]
        paired = stacked.reshape((4, count // 2, 2) + stacked.shape[2:])
        stacked = over(paired[:, :, 0], paired[:, :, 1])
    return stacked[:, 0]


def body(volume, view_side):
    ghosts = with_halo(volume, (("bx", 0), ("by", 1)), 1)
    width_x = volume.shape[0]
    width_y = volume.shape[1]
    depth = volume.shape[2]
    block_z = min(512, depth)
    ray_length = width_x * lax.axis_size("bx")
    padded = jnp.pad(ghosts, ((0, 0), (0, 0), (1, 1)))
    reversed_rows = (view_side == 1)[None, None, :, None]

    def render_block(block):
        start = block * block_z
        stencil = lax.dynamic_slice(
            padded, (jnp.int32(0), jnp.int32(0), start), (width_x + 2, width_y + 2, block_z + 2)
        ).astype(jnp.float32)
        samples = shade_block(stencil, ray_length)
        samples = jnp.where(reversed_rows, jnp.flip(samples, 1), samples)
        return fold_layers(samples)

    blocks = lax.map(render_block, jnp.arange(depth // block_z, dtype=jnp.int32))
    partial_value = jnp.transpose(blocks, (1, 2, 0, 3)).reshape(4, width_y, depth)
    layers = lax.all_to_all(partial_value[:, None], "bx", split_axis=3, concat_axis=1, tiled=True)
    layers = jnp.where(reversed_rows, jnp.flip(layers, 1), layers)
    result = fold_layers(layers)
    return jnp.concatenate([result[:3], 1.0 - result[3:]], 0)


def solution(mesh):
    placed = (P("bx", "by", None), P("by"))
    return jax.shard_map(
        body, mesh=mesh, in_specs=placed, out_specs=P(None, "by", "bx"), check_vma=False
    )
```

profile of v0, /device:TPU:225, one launch (start us, length us, event | category | flops | bytes accessed | tf_op | source)
XLA Modules:
  0.0 113.5 jit_solution(18402032469455518042)
XLA Ops:
  0.0 1.0 fusion.44
  1.0 3.8 %collective-permute-start = (bf16[1,32,2048]{2,1,0:T(8,128)(2,1)S(1)}, bf16[1,32,2048]{2,1,0:T(8,128)(2,1)S(1)}, u32[]{:S(2)}, u32[]{:S(2)}) collective-permute-start(bf16[1,32,2048]{2,1,0:T(8,128)(2,1)S(1)} %get-tuple-element.109), channel_id=1, source_target_pairs={{0,16},{16,32},{32,48},{48,64},{64,80},{80,96},{96,112},{112,128},... | collective-permute-start | bytes 393224 | tf_op jit(solution)/shard_map/ppermute | solution.py:14
  4.8 1.9 %collective-permute-start.1 = (bf16[1,32,2048]{2,1,0:T(8,128)(2,1)S(1)}, bf16[1,32,2048]{2,1,0:T(8,128)(2,1)S(1)}, u32[]{:S(2)}, u32[]{:S(2)}) collective-permute-start(bf16[1,32,2048]{2,1,0:T(8,128)(2,1)S(1)} %get-tuple-element.108), channel_id=1, source_target_pairs={{16,0},{32,16},{48,32},{64,48},{80,64},{96,80},{112,96},{128,112},... | collective-permute-start | bytes 393224 | tf_op jit(solution)/shard_map/ppermute | solution.py:15
  6.7 1.7 %constant_dynamic-update-slice_fusion.1 = bf16[18,32,2048]{2,1,0:T(8,128)(2,1)S(1)} fusion(bf16[18,32,2048]{2,1,0:T(8,128)(2,1)S(1)} %constant_dynamic-update-slice_fusion.2, bf16[16,32,2048]{2,1,0:T(8,128)(2,1)} %param.4), kind=kLoop, calls=%fused_computation.81 | loop fusion | bytes 4194304
  8.5 2.6 %collective-permute-done.1 = bf16[1,32,2048]{2,1,0:T(8,128)(2,1)S(1)} collective-permute-done((bf16[1,32,2048]{2,1,0:T(8,128)(2,1)S(1)}, bf16[1,32,2048]{2,1,0:T(8,128)(2,1)S(1)}, u32[]{:S(2)}, u32[]{:S(2)}) %collective-permute-start.1) | collective-permute-done | bytes 131104 | tf_op jit(solution)/shard_map/ppermute | solution.py:15
  11.1 1.4 %copy-done = bf16[18,32,2048]{2,1,0:T(8,128)(2,1)} copy-done((bf16[18,32,2048]{2,1,0:T(8,128)(2,1)}, bf16[18,32,2048]{2,1,0:T(8,128)(2,1)S(1)}, u32[]{:S(2)}) %copy-start) | copy-done | bytes 2359320
  12.5 0.2 fusion.41
  12.8 4.8 %collective-permute-start.2 = (bf16[18,1,2048]{2,1,0:T(2,128)(2,1)S(1)}, bf16[18,1,2048]{2,1,0:T(2,128)(2,1)S(1)}, u32[]{:S(2)}, u32[]{:S(2)}) collective-permute-start(bf16[18,1,2048]{2,1,0:T(2,128)(2,1)S(1)} %get-tuple-element.102), channel_id=1, source_target_pairs={{0,1},{1,2},{2,3},{3,4},{4,5},{5,6},{6,7},{7,8},{8,9},{9,10},{10,1... | collective-permute-start | bytes 221192 | tf_op jit(solution)/shard_map/ppermute | solution.py:14
  17.5 1.9 %collective-permute-start.3 = (bf16[18,1,2048]{2,1,0:T(2,128)(2,1)S(1)}, bf16[18,1,2048]{2,1,0:T(2,128)(2,1)S(1)}, u32[]{:S(2)}, u32[]{:S(2)}) collective-permute-start(bf16[18,1,2048]{2,1,0:T(2,128)(2,1)S(1)} %get-tuple-element.103), channel_id=1, source_target_pairs={{1,0},{2,1},{3,2},{4,3},{5,4},{6,5},{7,6},{8,7},{9,8},{10,9},{11,1... | collective-permute-start | bytes 221192 | tf_op jit(solution)/shard_map/ppermute | solution.py:15
  19.6 5.0 %collective-permute-done.3 = bf16[18,1,2048]{2,1,0:T(2,128)(2,1)S(1)} collective-permute-done((bf16[18,1,2048]{2,1,0:T(2,128)(2,1)S(1)}, bf16[18,1,2048]{2,1,0:T(2,128)(2,1)S(1)}, u32[]{:S(2)}, u32[]{:S(2)}) %collective-permute-start.3) | collective-permute-done | bytes 73760 | tf_op jit(solution)/shard_map/ppermute | solution.py:15
  24.6 4.6 %fusion.23 = bf16[18,34,2050]{2,1,0:T(8,128)(2,1)S(1)} fusion(bf16[18,1,2048]{2,1,0:T(2,128)(2,1)S(1)} %collective-permute-done.3, bf16[18,32,2048]{2,1,0:T(8,128)(2,1)} %copy-done, bf16[18,1,2048]{2,1,0:T(2,128)(2,1)S(1)} %collective-permute-done.2), kind=kLoop, calls=%fused_computation.52 | loop fusion | flops 15055200 | bytes 5015952 | tf_op jit(solution)/shard_map/concatenate | solution.py:16
  29.3 31.7 %while.12 = (s32[]{:T(128)}, f32[4,4,32,512]{3,2,1,0:T(8,128)}, pred[1,1,32,1]{2,3,1,0:T(4,128)(4,1)S(1)}, s32[4]{0:T(128)S(1)}, bf16[18,34,2050]{2,1,0:T(8,128)...) while((s32[]{:T(128)}, f32[4,4,32,512]{3,2,1,0:T(8,128)}, ...), condition=%wide.region_1.2_spmd, body=%wide.region_0.1_spmd.sunk | while | flops 17697996 | bytes 60346216 | solution.py:70
  29.3 0.6 dynamic_slice.17
  30.5 0.4 dynamic-slice_convert_fusion.2
  30.9 1.8 %multiply_bitcast_fusion.5 = (f32[1,16,32,512]{3,2,1,0:T(8,128)S(1)}, f32[16,32,512]{2,1,0:T(8,128)S(1)}, f32[16,32,512]{2,1,0:T(8,128)S(1)}) fusion(f32[18,34,514]{2,1,0:T(8,128)S(1)} %dynamic-slice_convert_fusion.2), kind=kLoop, calls=%fused_computation.20.clone.1 | loop fusion | flops 9175040 | bytes 10485760 | tf_op jit(solution)/shard_map/while/body/eval_jaxpr/stack | solution.py:35
  32.8 0.6 multiply_bitcast_fusion.6
  33.3 0.7 pad_maximum_fusion.3
  34.1 0.9 reverse_select_fusion.2
  35.0 0.3 fusion.63
  35.4 0.5 fusion.64
  36.5 0.7 fusion.69
  37.2 0.6 dynamic_slice.17
  38.5 0.4 dynamic-slice_convert_fusion.2
  38.8 1.8 %multiply_bitcast_fusion.5 = (f32[1,16,32,512]{3,2,1,0:T(8,128)S(1)}, f32[16,32,512]{2,1,0:T(8,128)S(1)}, f32[16,32,512]{2,1,0:T(8,128)S(1)}) fusion(f32[18,34,514]{2,1,0:T(8,128)S(1)} %dynamic-slice_convert_fusion.2), kind=kLoop, calls=%fused_computation.20.clone.1 | loop fusion | flops 9175040 | bytes 10485760 | tf_op jit(solution)/shard_map/while/body/eval_jaxpr/stack | solution.py:35
  40.7 0.6 multiply_bitcast_fusion.6
  41.3 0.7 pad_maximum_fusion.3
  42.0 0.9 reverse_select_fusion.2
  42.9 0.3 fusion.63
  43.3 0.5 fusion.64
  43.9 0.2 fusion.66
  44.4 0.8 fusion.69
  45.1 0.6 dynamic_slice.17
  46.4 0.4 dynamic-slice_convert_fusion.2
  46.8 1.8 %multiply_bitcast_fusion.5 = (f32[1,16,32,512]{3,2,1,0:T(8,128)S(1)}, f32[16,32,512]{2,1,0:T(8,128)S(1)}, f32[16,32,512]{2,1,0:T(8,128)S(1)}) fusion(f32[18,34,514]{2,1,0:T(8,128)S(1)} %dynamic-slice_convert_fusion.2), kind=kLoop, calls=%fused_computation.20.clone.1 | loop fusion | flops 9175040 | bytes 10485760 | tf_op jit(solution)/shard_map/while/body/eval_jaxpr/stack | solution.py:35
  48.6 0.6 multiply_bitcast_fusion.6
  49.2 0.7 pad_maximum_fusion.3
  49.9 0.9 reverse_select_fusion.2
  50.8 0.3 fusion.63
  51.2 0.5 fusion.64
  52.3 0.7 fusion.69
  53.0 0.6 dynamic_slice.17
  54.3 0.4 dynamic-slice_convert_fusion.2
  54.7 1.8 %multiply_bitcast_fusion.5 = (f32[1,16,32,512]{3,2,1,0:T(8,128)S(1)}, f32[16,32,512]{2,1,0:T(8,128)S(1)}, f32[16,32,512]{2,1,0:T(8,128)S(1)}) fusion(f32[18,34,514]{2,1,0:T(8,128)S(1)} %dynamic-slice_convert_fusion.2), kind=kLoop, calls=%fused_computation.20.clone.1 | loop fusion | flops 9175040 | bytes 10485760 | tf_op jit(solution)/shard_map/while/body/eval_jaxpr/stack | solution.py:35
  56.5 0.6 multiply_bitcast_fusion.6
  57.1 0.7 pad_maximum_fusion.3
  57.8 0.9 reverse_select_fusion.2
  58.7 0.3 fusion.63
  59.1 0.5 fusion.64
  60.2 0.7 fusion.69
  61.0 4.6 %copy.56 = f32[4,32,4,512]{1,0,3,2:T(4,128)} copy(f32[4,32,4,512]{3,1,0,2:T(8,128)} %bitcast.28) | data formatting | bytes 2097152 | tf_op jit(solution)/shard_map/broadcast_in_dim;reshape | solution.py:72
  65.5 4.4 %reshape.417 = f32[32,1,8192]{2,1,0:T(1,128)S(1)} reshape(f32[2048,1,4,32]{3,2,1,0:T(4,128)} %bitcast.219) | data formatting | bytes 2097152
  69.9 25.2 %all_to_all.18 = f32[32,1,8192]{2,1,0:T(1,128)S(1)} all-to-all(f32[32,1,8192]{2,1,0:T(1,128)S(1)} %reshape.417), channel_id=1, replica_groups=mesh['bx'=32,'by'=16] {'bx'}, dimensions={0} | all-to-all | bytes 2097152 | tf_op jit(solution)/shard_map/all_to_all | solution.py:72
  95.1 0.5 broadcast.169
  95.6 3.2 %reduce = f32[32,8192]{1,0:T(8,128)S(1)} reduce(f32[32,1,8192]{2,1,0:T(1,128)S(1)} %all_to_all.18, f32[]{:T(128)} %broadcast.169), dimensions={1}, to_apply=%all_to_all.13.reduce_sub_computation | reduce | bytes 2097156 | tf_op jit(solution)/shard_map/all_to_all | solution.py:72
  98.9 3.5 %reshape.418 = f32[2048,1,4,32]{3,2,1,0:T(4,128)} reshape(f32[32,8192]{1,0:T(8,128)S(1)} %reduce) | data formatting | bytes 2097152
  102.4 3.7 %copy.57 = f32[4,1,32,32,64]{4,3,2,0,1:T(8,128)S(1)} copy(f32[4,1,32,32,64]{2,0,4,3,1:T(4,128)} %bitcast.220) | data formatting | bytes 2097152 | tf_op jit(solution)/shard_map/all_to_all | solution.py:72
  106.0 2.0 %rev.11 = f32[4,32,32,64]{3,1,2,0:T(8,128)} reverse(f32[4,32,32,64]{3,1,2,0:T(8,128)S(1)} %bitcast.218), dimensions={1} | reverse | bytes 2097152 | tf_op jit(solution)/shard_map/jit(_flip)/rev | solution.py:73
  108.1 1.9 %broadcast_select_fusion = f32[4,32,32,64]{3,1,2,0:T(8,128)S(1)} fusion(f32[4,32,32,64]{3,1,2,0:T(8,128)} %rev.11, pred[32]{0:T(512)(128)(4,1)S(1)} %get-tuple-element.122, f32[4,1,32,32,64]{4,3,2,0,1:T(8,128)S(1)} %copy.57), kind=kLoop, calls=%fused_computation.53 | loop fusion | flops 262144 | bytes 3145760 | tf_op jit(solution)/shard_map/jit(_where)/select_n | solution.py:73
  109.9 0.4 fusion.43
  110.3 1.2 %fusion.42 = (f32[3,16,1,32,64]{4,2,1,3,0:T(1,128)S(1)}, f32[3,16,1,32,64]{4,2,1,3,0:T(1,128)S(1)}) fusion(f32[4,16,2,32,64]{4,2,1,3,0:T(2,128)S(1)} %bitcast.222), kind=kLoop, calls=%fused_computation.90 | loop fusion | bytes 1572864 | tf_op jit(solution)/shard_map/slice | solution.py:39
  111.8 0.3 copy.63
  112.1 0.3 copy.65
  112.3 0.2 multiply_add_fusion.1
  112.9 0.6 pad_maximum_fusion.1
  (62 shorter events, 2.9 us)
Async XLA Ops:
  1.0 5.7 %collective-permute-start = (bf16[1,32,2048]{2,1,0:T(8,128)(2,1)S(1)}, bf16[1,32,2048]{2,1,0:T(8,128)(2,1)S(1)}, u32[]{:S(2)}, u32[]{:S(2)}) collective-permute-start(bf16[1,32,2048]{2,1,0:T(8,128)(2,1)S(1)} %get-tuple-element.109), channel_id=1, source_target_pairs={{0,16},{16,32},{32,48},{48,64},{64,80},{80,96},{96,112},{112,128},... | collective-permute-start | bytes 393224 | tf_op jit(solution)/shard_map/ppermute | solution.py:14
  4.8 6.3 %collective-permute-start.1 = (bf16[1,32,2048]{2,1,0:T(8,128)(2,1)S(1)}, bf16[1,32,2048]{2,1,0:T(8,128)(2,1)S(1)}, u32[]{:S(2)}, u32[]{:S(2)}) collective-permute-start(bf16[1,32,2048]{2,1,0:T(8,128)(2,1)S(1)} %get-tuple-element.108), channel_id=1, source_target_pairs={{16,0},{32,16},{48,32},{64,48},{80,64},{96,80},{112,96},{128,112},... | collective-permute-start | bytes 393224 | tf_op jit(solution)/shard_map/ppermute | solution.py:15
  6.7 12.7 %copy-start.1 = (s32[32]{0:T(128)S(1)}, s32[32]{0:T(128)}, u32[]{:S(2)}) copy-start(s32[32]{0:T(128)} %param.5) | copy-start | bytes 388
  11.1 1.4 %copy-start = (bf16[18,32,2048]{2,1,0:T(8,128)(2,1)}, bf16[18,32,2048]{2,1,0:T(8,128)(2,1)S(1)}, u32[]{:S(2)}) copy-start(bf16[18,32,2048]{2,1,0:T(8,128)(2,1)S(1)} %constant_dynamic-update-slice_fusion) | copy-start | bytes 7077892
  12.8 6.8 %collective-permute-start.2 = (bf16[18,1,2048]{2,1,0:T(2,128)(2,1)S(1)}, bf16[18,1,2048]{2,1,0:T(2,128)(2,1)S(1)}, u32[]{:S(2)}, u32[]{:S(2)}) collective-permute-start(bf16[18,1,2048]{2,1,0:T(2,128)(2,1)S(1)} %get-tuple-element.102), channel_id=1, source_target_pairs={{0,1},{1,2},{2,3},{3,4},{4,5},{5,6},{6,7},{7,8},{8,9},{9,10},{10,1... | collective-permute-start | bytes 221192 | tf_op jit(solution)/shard_map/ppermute | solution.py:14
  17.5 7.1 %collective-permute-start.3 = (bf16[18,1,2048]{2,1,0:T(2,128)(2,1)S(1)}, bf16[18,1,2048]{2,1,0:T(2,128)(2,1)S(1)}, u32[]{:S(2)}, u32[]{:S(2)}) collective-permute-start(bf16[18,1,2048]{2,1,0:T(2,128)(2,1)S(1)} %get-tuple-element.103), channel_id=1, source_target_pairs={{1,0},{2,1},{3,2},{4,3},{5,4},{6,5},{7,6},{8,7},{9,8},{10,9},{11,1... | collective-permute-start | bytes 221192 | tf_op jit(solution)/shard_map/ppermute | solution.py:15
where the time goes:
time: 114 us
  other arithmetic  35.4 us (31%)
  local copies, waits for them, and re-layouts  29.5 us (26%)
  blocking collectives  25.2 us (22%)
  starting transfers between devices  12.4 us (11%)
  waiting for transfers between devices  7.72 us (7%)
  loops' own time  3.06 us (3%)
    all_to_all x1, blocking collectives, body(): lax.all_to_all(partial_value[:, None], 'bx', split_axis=3, concat_axis=1,...  25.2 us
    another operation x12, other arithmetic, shade_block(): jnp.stack([weight * red_part, weight * green_part, weight * blue_part, 1....  12.5 us
    unnamed x10, local copies, waits for them, and re-layouts  11.6 us
    ppermute x2, starting transfers between devices, with_halo(): before = lax.ppermute(last, axis, up)  8.52 us
    ppermute x2, waiting for transfers between devices, with_halo(): after = lax.ppermute(first, axis, down)  7.6 us
    concatenate x1, other arithmetic, with_halo(): x = jnp.concatenate([before, x, after], axis=dim)  4.63 us
    another operation x1, local copies, waits for them, and re-layouts, body(): partial_value[:, None]  4.57 us
    all_to_all x2, local copies, waits for them, and re-layouts, body(): lax.all_to_all(partial_value[:, None], 'bx', split_axis=3, concat_axis=1,...  4.19 us
  transfers between devices with their start and end apart: 4, of which 3 were waited for; matrix products, arithmetic and copies ran while one was open for 2% of the time, Pallas kernels for 0%

commit v1 on v0

v1 whole, which is shorter than its diff:
```python
import functools
import math

import jax
import jax.numpy as jnp
from jax import lax
from jax.experimental import pallas as pl
from jax.experimental.pallas import tpu as pltpu
from jax.sharding import PartitionSpec as P

F32 = jnp.float32
LANES = 128
TILES = 4
LOG2E = 1.0 / math.log(2.0)
FLOOR = -27.0
STEPS = 2621.0


def recip(x):
    return pl.reciprocal(x, approx=True)


def lane_tile(start):
    return pl.ds(pl.multiple_of(start, LANES), LANES)


def encode(value):
    level = jnp.log2(jnp.maximum(value, 2.0**FLOOR)) * STEPS + (0.5 - FLOOR * STEPS)
    return jnp.minimum(level, 65535.0).astype(jnp.int32) - 32768


def decode(code):
    code = code.astype(jnp.int32)
    value = jnp.exp2(code.astype(F32) * (1.0 / STEPS) + (32768.0 / STEPS + FLOOR))
    return jnp.where(code == -32768, 0.0, value)


def render_kernel(ray_length, vol, before, after, above, below, sign, codes, field, image):
    layers, rows, depth = vol.shape
    width = LANES * TILES
    chunks = depth // width
    scale = 3.0 / 1.2 / ray_length * LOG2E
    tone = math.sqrt(0.7)
    lane = lax.broadcasted_iota(jnp.int32, (8, LANES), 1)

    def chunk(c, carry):
        base = c * width

        def widen(l, carry):
            for t in range(TILES):
                field[l + 1, t + 1, pl.ds(8, rows), :] = vol[l, :, lane_tile(base + LANES * t)].astype(F32)
            left = lane_tile(jnp.maximum(base - LANES, 0))
            right = lane_tile(jnp.minimum(base + width, depth - LANES))
            field[l + 1, 0, pl.ds(8, rows), :] = jnp.where(c == 0, 0.0, vol[l, :, left].astype(F32))
            field[l + 1, TILES + 1, pl.ds(8, rows), :] = jnp.where(c == chunks - 1, 0.0, vol[l, :, right].astype(F32))
            return carry

        lax.fori_loop(0, layers, widen, 0, unroll=4)
        for t in range(TILES):
            here = lane_tile(base + LANES * t)
            field[pl.ds(1, layers), t + 1, 7, :] = above[:, here].astype(F32)
            field[pl.ds(1, layers), t + 1, rows + 8, :] = below[:, here].astype(F32)
            field[0, t + 1, pl.ds(8, rows), :] = before[0, :, here].astype(F32)
            field[layers + 1, t + 1, pl.ds(8, rows), :] = after[0, :, here].astype(F32)

        def row_block(r, carry):
            r8 = pl.multiple_of(8 * r, 8)
            side = sign[pl.ds(r8, 8), :]
            most = side * (1.25 * scale)
            part = side * scale
            path = [jnp.zeros((8, LANES), F32) for _ in range(TILES)]
            reach = [jnp.ones((8, LANES), F32) for _ in range(TILES)]
            color = [[jnp.zeros((8, LANES), F32) for _ in range(TILES)] for _ in range(3)]
            for l in range(layers):
                mid = [field[l + 1, t, pl.ds(r8 + 8, 8), :] for t in range(TILES + 2)]
                from_left = [pltpu.roll(v, 1, 1) for v in mid[:-1]]
                from_right = [pltpu.roll(v, LANES - 1, 1) for v in mid[1:]]
                for t in range(TILES):
                    v = mid[t + 1]
                    gz = jnp.where(lane == LANES - 1, from_right[t + 1], from_right[t]) - jnp.where(
                        lane == 0, from_left[t], from_left[t + 1]
                    )
                    gy = field[l + 1, t + 1, pl.ds(r8 + 9, 8), :] - field[l + 1, t + 1, pl.ds(r8 + 7, 8), :]
                    gx = field[l + 2, t + 1, pl.ds(r8 + 8, 8), :] - field[l, t + 1, pl.ds(r8 + 8, 8), :]
                    square = gx * gx + gy * gy + gz * gz
                    facing = (0.48 * tone) * gx + (0.6 * tone) * gy + (0.64 * tone) * gz
                    shading = 0.3 + facing * facing * recip(square + 4.0)
                    density = jnp.clip(v - 0.4, 0.0, 1.2)
                    path[t] = path[t] + density * (most - part * recip(square + 1.0))
                    next_reach = jnp.exp2(path[t])
                    weight = (next_reach - reach[t]) * shading
                    reach[t] = next_reach
                    color[0][t] = color[0][t] + weight * jnp.clip(v - 0.8, 0.0, 1.0)
                    color[1][t] = color[1][t] + weight * jnp.minimum(v, 2.0 - v)
                    color[2][t] = color[2][t] + weight * jnp.clip(1.2 - v, 0.0, 1.0)
            for t in range(TILES):
                here = lane_tile(base + LANES * t)
                factor = jnp.where(side > 0, jnp.exp2(-path[t]), -1.0)
                for k in range(3):
                    image[k, pl.ds(r8, 8), here] = color[k][t] * factor
                image[3, pl.ds(r8, 8), here] = path[t] * side
            return carry

        lax.fori_loop(0, rows // 8, row_block, 0)
        return carry

    lax.fori_loop(0, chunks, chunk, 0)
    half = rows // 2
    low = lax.broadcasted_iota(jnp.int32, (half, LANES), 1) < LANES // 2

    def pack(z, carry):
        here = lane_tile(LANES * z)
        for k in range(4):
            top = encode(image[k, pl.ds(0, half), here])
            bottom = encode(image[k, pl.ds(half, half), here])
            codes[2 * z, k] = jnp.where(low, top, pltpu.roll(bottom, LANES // 2, 1)).astype(jnp.int16)
            codes[2 * z + 1, k] = jnp.where(low, pltpu.roll(top, LANES // 2, 1), bottom).astype(jnp.int16)
        return carry

    lax.fori_loop(0, depth // LANES, pack, 0, unroll=2)


def fold_kernel(codes, sign, out):
    bricks, _, half, _ = codes.shape
    side = sign[...]
    backward = side > 0
    path = jnp.zeros((half, LANES), F32)
    color = [jnp.zeros((half, LANES), F32) for _ in range(3)]
    for k in range(bricks):
        farther = path + decode(codes[k, 3])
        reach = jnp.exp2(side * jnp.where(backward, farther, path))
        path = farther
        for q in range(3):
            color[q] = color[q] + reach * decode(codes[k, q])
    passing = jnp.exp2(-path)
    factor = jnp.where(backward, passing, 1.0)
    parts = [c * factor for c in color] + [1.0 - passing]
    for q in range(4):
        out[q, pl.ds(0, half), :] = parts[q][:, : LANES // 2]
        out[q, pl.ds(half, half), :] = parts[q][:, LANES // 2 :]


def body(volume, view_side):
    layers, rows, depth = volume.shape
    size_x, size_y = lax.axis_size("bx"), lax.axis_size("by")
    up_x = [(i, i + 1) for i in range(size_x - 1)]
    up_y = [(i, i + 1) for i in range(size_y - 1)]
    down_x = [(j, i) for i, j in up_x]
    down_y = [(j, i) for i, j in up_y]
    above = lax.ppermute(volume[:, rows - 1, :], "by", up_y)
    below = lax.ppermute(volume[:, 0, :], "by", down_y)
    before = lax.ppermute(volume[layers - 1 :], "bx", up_x)
    after = lax.ppermute(volume[:1], "bx", down_x)
    side = jnp.where(view_side == 1, 1.0, -1.0).astype(F32)
    sign = jnp.broadcast_to(side[:, None], (rows, LANES))
    half = rows // 2
    both = jnp.concatenate([sign[:half, : LANES // 2], sign[half:, : LANES // 2]], 1)
    in_vmem = pl.BlockSpec(memory_space=pltpu.VMEM)
    codes = pl.pallas_call(
        functools.partial(render_kernel, layers * size_x),
        out_shape=jax.ShapeDtypeStruct((size_x, 4, half, LANES), jnp.int16),
        in_specs=[in_vmem] * 6,
        out_specs=in_vmem,
        scratch_shapes=[
            pltpu.VMEM((layers + 2, TILES + 2, rows + 16, LANES), F32),
            pltpu.VMEM((4, rows, depth), F32),
        ],
        compiler_params=pltpu.CompilerParams(vmem_limit_bytes=40 << 20),
        name="render",
    )(volume, before, after, above, below, sign)
    codes = lax.all_to_all(codes, "bx", split_axis=0, concat_axis=0, tiled=True)
    return pl.pallas_call(
        fold_kernel,
        out_shape=jax.ShapeDtypeStruct((4, rows, depth // size_x), F32),
        in_specs=[in_vmem] * 2,
        out_specs=in_vmem,
        compiler_params=pltpu.CompilerParams(vmem_limit_bytes=32 << 20),
        name="fold",
    )(codes, both)


def solution(mesh):
    placed = (P("bx", "by", None), P("by"))
    return jax.shard_map(body, mesh=mesh, in_specs=placed, out_specs=P(None, "by", "bx"), check_vma=False)
```

time: 114 us -> 52.9 us (0.46)
  other arithmetic: 35.4 us -> 0.74 us
  blocking collectives: 25.2 us -> 0 us
  local copies, waits for them, and re-layouts: 29.5 us -> 4.36 us
  Pallas kernels: 0 us -> 11 us
  starting transfers between devices: 12.4 us -> 21.4 us
  waiting for transfers between devices: 7.72 us -> 15 us
  loops' own time: 3.06 us -> 0 us
    all_to_all x1 -> x0, blocking collectives: 25.2 us -> none  [body(): lax.all_to_all(partial_value[:, None], 'bx', split_axis=3, concat_axis=1,...]
    another operation x12 -> x0, other arithmetic: 12.5 us -> none  [shade_block(): jnp.stack([weight * red_part, weight * green_part, weight * blue_part, 1....]
    all_to_all x0 -> x1, waiting for transfers between devices: none -> 11.3 us  [body(): codes = lax.all_to_all(codes, 'bx', split_axis=0, concat_axis=0, tiled=True)]
    pallas_call x0 -> x2, Pallas kernels: none -> 11 us  [the longest x1 9.99 us: body(): pl.pallas_call(functools.partial(render_kernel, layers * size_x), out_sha...]
    unnamed x10 -> x4, local copies, waits for them, and re-layouts: 11.6 us -> 1.68 us
    all_to_all x0 -> x1, starting transfers between devices: none -> 9.06 us  [body(): codes = lax.all_to_all(codes, 'bx', split_axis=0, concat_axis=0, tiled=True)]
    concatenate x2 -> x1, other arithmetic: 5.27 us -> 0.08 us  [body(): jnp.concatenate([sign[:half, :LANES // 2], sign[half:, :LANES // 2]], 1)]
    select_n x5 -> x1, other arithmetic: 5.47 us -> 0.66 us  [body(): side = jnp.where(view_side == 1, 1.0, -1.0).astype(F32)]
  transfers between devices with their start and end apart: 4 -> 5, of which waited for: 3 -> 2; matrix products, arithmetic and copies ran while one was open for 2% -> 5% of each run, Pallas kernels for 0% -> 0%
where the time goes in v1:
time: 52.9 us; the launch traced here: 52.6 us
  starting transfers between devices  21.4 us (40%)
  waiting for transfers between devices  15 us (28%)
  Pallas kernels  11 us (21%)
  local copies, waits for them, and re-layouts  4.36 us (8%)
  other arithmetic  0.74 us (1%)
    all_to_all x1, waiting for transfers between devices, body(): codes = lax.all_to_all(codes, 'bx', split_axis=0, concat_axis=0, tiled=True)  11.3 us
    pallas_call x1, Pallas kernels, body(): pl.pallas_call(functools.partial(render_kernel, layers * size_x), out_sha...  9.99 us
    all_to_all x1, starting transfers between devices, body(): codes = lax.all_to_all(codes, 'bx', split_axis=0, concat_axis=0, tiled=True)  9.06 us
    ppermute x1, starting transfers between devices, body(): above = lax.ppermute(volume[:, rows - 1, :], 'by', up_y)  4.76 us
    ppermute x1, starting transfers between devices, body(): before = lax.ppermute(volume[layers - 1:], 'bx', up_x)  3.77 us
    ppermute x1, waiting for transfers between devices, body(): below = lax.ppermute(volume[:, 0, :], 'by', down_y)  3.63 us
    ppermute x1, starting transfers between devices, body(): below = lax.ppermute(volume[:, 0, :], 'by', down_y)  1.92 us
    ppermute x1, starting transfers between devices, body(): after = lax.ppermute(volume[:1], 'bx', down_x)  1.92 us
  transfers between devices with their start and end apart: 5, of which 2 were waited for; matrix products, arithmetic and copies ran while one was open for 5% of the time, Pallas kernels for 0%

profile of v1, /device:TPU:225, one launch (start us, length us, event | category | flops | bytes accessed | tf_op | source)
XLA Modules:
  0.0 52.6 jit_solution(8663672816914511164)
XLA Ops:
  0.0 1.0 %fusion.1 = (bf16[1,32,2048]{2,1,0:T(8,128)(2,1)S(1)}, bf16[1,32,2048]{2,1,0:T(8,128)(2,1)S(1)}) fusion(bf16[16,32,2048]{2,1,0:T(8,128)(2,1)} %vol.1), kind=kLoop, calls=%fused_computation.5 | loop fusion | bytes 524288 | tf_op jit(solution)/shard_map/slice | solution.py:153
  1.0 3.8 %collective-permute-start = (bf16[1,32,2048]{2,1,0:T(8,128)(2,1)S(1)}, bf16[1,32,2048]{2,1,0:T(8,128)(2,1)S(1)}, u32[]{:S(2)}, u32[]{:S(2)}) collective-permute-start(bf16[1,32,2048]{2,1,0:T(8,128)(2,1)S(1)} %get-tuple-element.8), channel_id=1, source_target_pairs={{0,16},{16,32},{32,48},{48,64},{64,80},{80,96},{96,112},{112,128},... | collective-permute-start | bytes 393224 | tf_op jit(solution)/shard_map/ppermute | solution.py:152
  4.8 1.9 %collective-permute-start.1 = (bf16[1,32,2048]{2,1,0:T(8,128)(2,1)S(1)}, bf16[1,32,2048]{2,1,0:T(8,128)(2,1)S(1)}, u32[]{:S(2)}, u32[]{:S(2)}) collective-permute-start(bf16[1,32,2048]{2,1,0:T(8,128)(2,1)S(1)} %get-tuple-element.7), channel_id=1, source_target_pairs={{16,0},{32,16},{48,32},{64,48},{80,64},{96,80},{112,96},{128,112},... | collective-permute-start | bytes 393224 | tf_op jit(solution)/shard_map/ppermute | solution.py:153
  6.7 1.4 %fusion = (bf16[16,1,2048]{2,1,0:T(2,128)(2,1)S(1)}, bf16[16,1,2048]{2,1,0:T(2,128)(2,1)S(1)}) fusion(bf16[16,32,2048]{2,1,0:T(8,128)(2,1)} %vol.1), kind=kLoop, calls=%fused_computation.4 | loop fusion | bytes 262144 | tf_op jit(solution)/shard_map/slice | solution.py:151
  8.2 4.8 %collective-permute-start.2 = (bf16[16,2048]{1,0:T(8,128)(2,1)S(1)}, bf16[16,2048]{1,0:T(8,128)(2,1)S(1)}, u32[]{:S(2)}, u32[]{:S(2)}) collective-permute-start(bf16[16,2048]{1,0:T(8,128)(2,1)S(1)} %bitcast.6), channel_id=1, source_target_pairs={{0,1},{1,2},{2,3},{3,4},{4,5},{5,6},{6,7},{7,8},{8,9},{9,10},{10,1... | collective-permute-start | bytes 196616 | tf_op jit(solution)/shard_map/ppermute | solution.py:150
  13.0 1.9 %collective-permute-start.3 = (bf16[16,2048]{1,0:T(8,128)(2,1)S(1)}, bf16[16,2048]{1,0:T(8,128)(2,1)S(1)}, u32[]{:S(2)}, u32[]{:S(2)}) collective-permute-start(bf16[16,2048]{1,0:T(8,128)(2,1)S(1)} %bitcast.7), channel_id=1, source_target_pairs={{1,0},{2,1},{3,2},{4,3},{5,4},{6,5},{7,6},{8,7},{9,8},{10,9},{11,1... | collective-permute-start | bytes 196616 | tf_op jit(solution)/shard_map/ppermute | solution.py:151
  14.9 0.7 %compare_select_fusion = f32[32]{0:T(128)S(1)} fusion(s32[32]{0:T(128)} %param.3), kind=kLoop, calls=%fused_computation.3 | loop fusion | flops 64 | bytes 256 | tf_op jit(solution)/shard_map/jit(_where)/select_n | solution.py:154
  15.6 0.0 collective-permute-done.2.above
  15.6 3.6 %collective-permute-done.3.below = bf16[16,2048]{1,0:T(8,128)(2,1)S(1)} collective-permute-done((bf16[16,2048]{1,0:T(8,128)(2,1)S(1)}, bf16[16,2048]{1,0:T(8,128)(2,1)S(1)}, u32[]{:S(2)}, u32[]{:S(2)}) %collective-permute-start.3) | collective-permute-done | bytes 65568 | tf_op jit(solution)/shard_map/ppermute | solution.py:151
  19.2 0.0 collective-permute-done.before
  19.2 0.0 collective-permute-done.1.after
  19.2 0.1 broadcast_in_dim.20.sign
  19.3 0.0 copy-start
  19.3 1.6 %copy-done = bf16[16,32,2048]{2,1,0:T(8,128)(2,1)S(1)} copy-done((bf16[16,32,2048]{2,1,0:T(8,128)(2,1)S(1)}, bf16[16,32,2048]{2,1,0:T(8,128)(2,1)}, u32[]{:S(2)}) %copy-start) | copy-done | bytes 2097176
  20.9 10.0 %render.1 = s16[32,4,16,128]{3,2,1,0:T(8,128)(2,1)} custom-call(bf16[16,32,2048]{2,1,0:T(8,128)(2,1)S(1)} %copy-done, bf16[1,32,2048]{2,1,0:T(8,128)(2,1)S(1)} %collective-permute-done.before, bf16[1,32,2048]{2,1,0:T(8,128)(2,1)S(1)} %collective-permute-done.1.after, bf16[16,2048]{1,0:T(8,128)(2,1)S(1)} %collective-permute-done.2.above, ...), custom_call_target="tpu_custom_call" | custom-call | tf_op jit(solution)/shard_map/render/pallas_call | solution.py:159
  30.9 9.1 %all-to-all-start = ((s16[32,4,16,128]{3,2,1,0:T(8,128)(2,1)}), s16[32,4,16,128]{3,2,1,0:T(8,128)(2,1)S(1)}, u32[]{:S(2)}, u32[]{:S(2)}) async-start(s16[32,4,16,128]{3,2,1,0:T(8,128)(2,1)} %render.1), calls=%async_computation | async-start | bytes 1048576 | tf_op jit(solution)/shard_map/all_to_all | solution.py:171
  39.9 0.1 fusion.2
  40.0 0.1 broadcast_in_dim.21
  40.1 0.1 broadcast_in_dim.22
  40.1 0.1 pad_maximum_fusion.sign
  40.2 11.3 %all-to-all-done.codes = s16[32,4,16,128]{3,2,1,0:T(8,128)(2,1)S(1)} async-done(((s16[32,4,16,128]{3,2,1,0:T(8,128)(2,1)}), s16[32,4,16,128]{3,2,1,0:T(8,128)(2,1)S(1)}, u32[]{:S(2)}, u32[]{:S(2)}) %all-to-all-start) | async-done | bytes 524320 | tf_op jit(solution)/shard_map/all_to_all | solution.py:171
  51.6 1.0 %fold.1 = f32[4,32,64]{2,1,0:T(8,128)} custom-call(s16[32,4,16,128]{3,2,1,0:T(8,128)(2,1)S(1)} %all-to-all-done.codes, f32[16,128]{1,0:T(8,128)S(1)} %pad_maximum_fusion.sign), custom_call_target="tpu_custom_call" | custom-call | tf_op jit(solution)/shard_map/fold/pallas_call | solution.py:172
  (2 shorter events, 0.1 us)
Async XLA Ops:
  1.0 18.2 %collective-permute-start = (bf16[1,32,2048]{2,1,0:T(8,128)(2,1)S(1)}, bf16[1,32,2048]{2,1,0:T(8,128)(2,1)S(1)}, u32[]{:S(2)}, u32[]{:S(2)}) collective-permute-start(bf16[1,32,2048]{2,1,0:T(8,128)(2,1)S(1)} %get-tuple-element.8), channel_id=1, source_target_pairs={{0,16},{16,32},{32,48},{48,64},{64,80},{80,96},{96,112},{112,128},... | collective-permute-start | bytes 393224 | tf_op jit(solution)/shard_map/ppermute | solution.py:152
  4.8 14.4 %collective-permute-start.1 = (bf16[1,32,2048]{2,1,0:T(8,128)(2,1)S(1)}, bf16[1,32,2048]{2,1,0:T(8,128)(2,1)S(1)}, u32[]{:S(2)}, u32[]{:S(2)}) collective-permute-start(bf16[1,32,2048]{2,1,0:T(8,128)(2,1)S(1)} %get-tuple-element.7), channel_id=1, source_target_pairs={{16,0},{32,16},{48,32},{64,48},{80,64},{96,80},{112,96},{128,112},... | collective-permute-start | bytes 393224 | tf_op jit(solution)/shard_map/ppermute | solution.py:153
  8.2 7.4 %collective-permute-start.2 = (bf16[16,2048]{1,0:T(8,128)(2,1)S(1)}, bf16[16,2048]{1,0:T(8,128)(2,1)S(1)}, u32[]{:S(2)}, u32[]{:S(2)}) collective-permute-start(bf16[16,2048]{1,0:T(8,128)(2,1)S(1)} %bitcast.6), channel_id=1, source_target_pairs={{0,1},{1,2},{2,3},{3,4},{4,5},{5,6},{6,7},{7,8},{8,9},{9,10},{10,1... | collective-permute-start | bytes 196616 | tf_op jit(solution)/shard_map/ppermute | solution.py:150
  13.0 6.2 %collective-permute-start.3 = (bf16[16,2048]{1,0:T(8,128)(2,1)S(1)}, bf16[16,2048]{1,0:T(8,128)(2,1)S(1)}, u32[]{:S(2)}, u32[]{:S(2)}) collective-permute-start(bf16[16,2048]{1,0:T(8,128)(2,1)S(1)} %bitcast.7), channel_id=1, source_target_pairs={{1,0},{2,1},{3,2},{4,3},{5,4},{6,5},{7,6},{8,7},{9,8},{10,9},{11,1... | collective-permute-start | bytes 196616 | tf_op jit(solution)/shard_map/ppermute | solution.py:151
  19.3 1.6 %copy-start = (bf16[16,32,2048]{2,1,0:T(8,128)(2,1)S(1)}, bf16[16,32,2048]{2,1,0:T(8,128)(2,1)}, u32[]{:S(2)}) copy-start(bf16[16,32,2048]{2,1,0:T(8,128)(2,1)} %vol.1) | copy-start | bytes 6291460
  30.9 20.7 %all-to-all-start = ((s16[32,4,16,128]{3,2,1,0:T(8,128)(2,1)}), s16[32,4,16,128]{3,2,1,0:T(8,128)(2,1)S(1)}, u32[]{:S(2)}, u32[]{:S(2)}) async-start(s16[32,4,16,128]{3,2,1,0:T(8,128)(2,1)} %render.1), calls=%async_computation | async-start | bytes 1048576 | tf_op jit(solution)/shard_map/all_to_all | solution.py:171

commit v2 on v1

v2 whole, which is shorter than its diff:
```python
import functools
import math

import jax
import jax.numpy as jnp
from jax import lax
from jax.experimental import pallas as pl
from jax.experimental.pallas import tpu as pltpu
from jax.sharding import PartitionSpec as P

F32 = jnp.float32
BF16 = jnp.bfloat16
LANES = 128
TILES = 4
LOG2E = 1.0 / math.log(2.0)
FLOOR = -27.0
STEPS = 2621.0
TONE = 0.7 * 0.48 * 0.48


def recip(x):
    return pl.reciprocal(x, approx=True)


def lane_tile(start):
    return pl.ds(pl.multiple_of(start, LANES), LANES)


def encode(value):
    level = jnp.log2(jnp.maximum(value, 2.0**FLOOR)) * STEPS + (0.5 - FLOOR * STEPS)
    return jnp.minimum(level, 65535.0).astype(jnp.int32) - 32768


def decode(code):
    code = code.astype(jnp.int32)
    value = jnp.exp2(code.astype(F32) * (1.0 / STEPS) + (32768.0 / STEPS + FLOOR))
    return jnp.where(code == -32768, 0.0, value)


def side_column(view):
    rows = view.shape[1]
    spread = jnp.broadcast_to(view[...].astype(F32), (rows, rows))
    down = lax.broadcasted_iota(jnp.int32, (rows, rows), 0)
    along = lax.broadcasted_iota(jnp.int32, (rows, rows), 1)
    picked = jnp.sum(jnp.where(down == along, spread, 0.0), axis=1, keepdims=True)
    return jnp.where(picked > 0.5, 1.0, -1.0)


def edge_kernel(vol, first_row, last_row, first_layer, last_layer):
    layers, rows, depth = vol.shape

    def tile(z, carry):
        here = lane_tile(LANES * z)
        first_row[:, here] = jnp.concatenate([vol[l, :, here].astype(F32)[:1] for l in range(layers)], 0).astype(BF16)
        last_row[:, here] = jnp.concatenate([vol[l, :, here].astype(F32)[rows - 1 :] for l in range(layers)], 0).astype(BF16)
        first_layer[:, here] = vol[0, :, here]
        last_layer[:, here] = vol[layers - 1, :, here]
        return carry

    lax.fori_loop(0, depth // LANES, tile, 0, unroll=2)


class Sweep:
    def __init__(self, vol, fields, ray_length, halo=None):
        self.vol, self.fields, self.halo = vol, fields, halo
        self.layers, self.rows, self.depth = vol.shape
        self.width = LANES * TILES
        self.chunks = self.depth // self.width
        self.scale = 3.0 / 1.2 / ray_length * LOG2E
        self.lane = lax.broadcasted_iota(jnp.int32, (8, LANES), 1)

    def widen_layer(self, field, c, l):
        base = c * self.width
        inside = pl.ds(8, self.rows)
        for t in range(TILES):
            field[l + 1, t + 1, inside, :] = self.vol[l, :, lane_tile(base + LANES * t)].astype(F32)
        left = lane_tile(jnp.maximum(base - LANES, 0))
        right = lane_tile(jnp.minimum(base + self.width, self.depth - LANES))
        field[l + 1, 0, inside, :] = jnp.where(c == 0, 0.0, self.vol[l, :, left].astype(F32))
        field[l + 1, TILES + 1, inside, :] = jnp.where(c == self.chunks - 1, 0.0, self.vol[l, :, right].astype(F32))

    def widen_halo(self, field, c, t):
        before, after, above, below = self.halo
        here = lane_tile(c * self.width + LANES * t)
        inside = pl.ds(8, self.rows)
        field[0, t + 1, inside, :] = before[:, here].astype(F32)
        field[self.layers + 1, t + 1, inside, :] = after[:, here].astype(F32)
        field[pl.ds(1, self.layers), t + 1, 7, :] = above[:, here].astype(F32)
        field[pl.ds(1, self.layers), t + 1, self.rows + 8, :] = below[:, here].astype(F32)

    def quarter(self, field, c, p):
        each = self.layers // 4
        tasks = [functools.partial(self.widen_layer, field, c, each * p + k) for k in range(each)]
        if self.halo is not None:
            tasks.append(functools.partial(self.widen_halo, field, c, p))
        return tasks

    def fresh(self):
        return dict(
            path=[jnp.zeros((8, LANES), F32) for _ in range(TILES)],
            reach=[jnp.ones((8, LANES), F32) for _ in range(TILES)],
            color=[[jnp.zeros((8, LANES), F32) for _ in range(TILES)] for _ in range(4)],
        )

    def layer(self, field, r8, side, state, l):
        lane = self.lane
        most, part = side * (1.25 * self.scale), side * self.scale
        path, reach, color = state["path"], state["reach"], state["color"]
        mid = [field[l + 1, t, pl.ds(r8 + 8, 8), :] for t in range(TILES + 2)]
        from_left = [pltpu.roll(v, 1, 1) for v in mid[:-1]]
        from_right = [pltpu.roll(v, LANES - 1, 1) for v in mid[1:]]
        for t in range(TILES):
            v = mid[t + 1]
            gz = jnp.where(lane == LANES - 1, from_right[t + 1], from_right[t]) - jnp.where(
                lane == 0, from_left[t], from_left[t + 1]
            )
            gy = field[l + 1, t + 1, pl.ds(r8 + 9, 8), :] - field[l + 1, t + 1, pl.ds(r8 + 7, 8), :]
            gx = field[l + 2, t + 1, pl.ds(r8 + 8, 8), :] - field[l, t + 1, pl.ds(r8 + 8, 8), :]
            square = gx * gx + gy * gy + gz * gz
            facing = gx + (0.6 / 0.48) * gy + (0.64 / 0.48) * gz
            shading = 0.3 / TONE + facing * facing * recip(square + 4.0)
            density = jnp.clip(v - 0.4, 0.0, 1.2)
            path[t] = path[t] + density * (most - part * recip(square + 1.0))
            next_reach = jnp.exp2(path[t])
            weight = (next_reach - reach[t]) * shading
            reach[t] = next_reach
            color[0][t] = color[0][t] + weight * jnp.clip(v, 0.8, 1.8)
            color[1][t] = color[1][t] + weight * jnp.minimum(v, 2.0 - v)
            color[2][t] = color[2][t] + weight * jnp.clip(v, 0.2, 1.2)
            color[3][t] = color[3][t] + weight

    def run(self, work):
        even, odd = self.fields
        for p in range(4):
            for task in self.quarter(even, 0, p):
                task()

        def pair(k, carry):
            for now, later, c in ((even, odd, 2 * k), (odd, even, 2 * k + 1)):
                following = jnp.minimum(c + 1, self.chunks - 1)

                def half(q, carry, now=now, later=later, c=c, following=following):
                    tasks = self.quarter(later, following, 2 * q) + self.quarter(later, following, 2 * q + 1)
                    work(now, c, q, tasks)
                    return carry

                lax.fori_loop(0, 2, half, 0)
            return carry

        lax.fori_loop(0, self.chunks // 2, pair, 0)


def inner_kernel(ray_length, vol, view, part, even, odd, sign):
    sweep = Sweep(vol, (even, odd), ray_length)
    rows = sweep.rows
    sign[...] = jnp.broadcast_to(side_column(view), (rows, LANES))

    def work(field, c, q, tasks):
        r8 = pl.multiple_of(8 + 8 * q, 8)
        side = sign[pl.ds(r8, 8), :]
        state = sweep.fresh()
        for l in range(1, sweep.layers - 1):
            sweep.layer(field, r8, side, state, l)
            if tasks:
                tasks.pop(0)()
        while tasks:
            tasks.pop(0)()
        for t in range(TILES):
            here = lane_tile(c * sweep.width + LANES * t)
            for k, kind in enumerate([state["path"]] + state["color"]):
                part[k, pl.ds(pl.multiple_of(8 * q, 8), 8), here] = kind[t]

    sweep.run(work)


def outer_kernel(ray_length, vol, before, after, above, below, view, part, codes, even, odd, sign, image):
    sweep = Sweep(vol, (even, odd), ray_length, (before, after, above, below))
    layers, rows, depth = vol.shape
    sign[...] = jnp.broadcast_to(side_column(view), (rows, LANES))

    def finish(c, r8, side, state):
        for t in range(TILES):
            here = lane_tile(c * sweep.width + LANES * t)
            path = state["path"][t]
            red, green, blue, total = (kind[t] for kind in state["color"])
            factor = jnp.where(side > 0, jnp.exp2(-path), -1.0) * TONE
            image[0, pl.ds(r8, 8), here] = (red - 0.8 * total) * factor
            image[1, pl.ds(r8, 8), here] = green * factor
            image[2, pl.ds(r8, 8), here] = (1.2 * total - blue) * factor
            image[3, pl.ds(r8, 8), here] = path * side

    def work(field, c, q, tasks):
        r8 = pl.multiple_of(24 * q, 8)
        side = sign[pl.ds(r8, 8), :]
        state = sweep.fresh()
        for l in range(layers):
            sweep.layer(field, r8, side, state, l)
            if tasks:
                tasks.pop(0)()
        while tasks:
            tasks.pop(0)()
        finish(c, r8, side, state)
        r8 = pl.multiple_of(8 + 8 * q, 8)
        side = sign[pl.ds(r8, 8), :]
        state = sweep.fresh()
        sweep.layer(field, r8, side, state, 0)
        for t in range(TILES):
            here = lane_tile(c * sweep.width + LANES * t)
            block = [part[k, pl.ds(pl.multiple_of(8 * q, 8), 8), here] for k in range(5)]
            for k in range(4):
                state["color"][k][t] = state["color"][k][t] + state["reach"][t] * block[k + 1]
            state["path"][t] = state["path"][t] + block[0]
            state["reach"][t] = jnp.exp2(state["path"][t])
        sweep.layer(field, r8, side, state, layers - 1)
        finish(c, r8, side, state)

    sweep.run(work)
    half = rows // 2
    low = lax.broadcasted_iota(jnp.int32, (half, LANES), 1) < LANES // 2

    def pack(z, carry):
        here = lane_tile(LANES * z)
        for k in range(4):
            top = encode(image[k, pl.ds(0, half), here])
            bottom = encode(image[k, pl.ds(half, half), here])
            codes[2 * z, k] = jnp.where(low, top, pltpu.roll(bottom, LANES // 2, 1)).astype(jnp.int16)
            codes[2 * z + 1, k] = jnp.where(low, pltpu.roll(top, LANES // 2, 1), bottom).astype(jnp.int16)
        return carry

    lax.fori_loop(0, depth // LANES, pack, 0, unroll=2)


def fold_kernel(codes, view, out):
    bricks, _, half, _ = codes.shape
    column = side_column(view)
    low = lax.broadcasted_iota(jnp.int32, (half, LANES), 1) < LANES // 2
    side = jnp.where(low, column[:half], column[half:])
    backward = side > 0
    path = jnp.zeros((half, LANES), F32)
    color = [jnp.zeros((half, LANES), F32) for _ in range(3)]
    for k in range(bricks):
        farther = path + decode(codes[k, 3])
        reach = jnp.exp2(side * jnp.where(backward, farther, path))
        path = farther
        for q in range(3):
            color[q] = color[q] + reach * decode(codes[k, q])
    passing = jnp.exp2(-path)
    factor = jnp.where(backward, passing, 1.0)
    parts = [c * factor for c in color] + [1.0 - passing]
    for q in range(4):
        out[q, pl.ds(0, half), :] = parts[q][:, : LANES // 2]
        out[q, pl.ds(half, half), :] = parts[q][:, LANES // 2 :]


def body(volume, view_side):
    layers, rows, depth = volume.shape
    size_x, size_y = lax.axis_size("bx"), lax.axis_size("by")
    up_x = [(i, i + 1) for i in range(size_x - 1)]
    up_y = [(i, i + 1) for i in range(size_y - 1)]
    down_x = [(j, i) for i, j in up_x]
    down_y = [(j, i) for i, j in up_y]
    view = view_side[None, :]
    half = rows // 2
    in_vmem = pl.BlockSpec(memory_space=pltpu.VMEM)
    shape = jax.ShapeDtypeStruct

    def call(kernel, operands, out_shape, scratch, name, cost=None, limit=24):
        return pl.pallas_call(
            kernel,
            out_shape=out_shape,
            in_specs=[in_vmem] * len(operands),
            out_specs=jax.tree.map(lambda _: in_vmem, out_shape),
            scratch_shapes=scratch,
            compiler_params=pltpu.CompilerParams(vmem_limit_bytes=limit << 20),
            cost_estimate=cost,
            name=name,
        )(*operands)

    field = pltpu.VMEM((layers + 2, TILES + 2, rows + 16, LANES), F32)
    sign = pltpu.VMEM((rows, LANES), F32)
    row, layer = shape((layers, depth), BF16), shape((rows, depth), BF16)
    first_row, last_row, first_layer, last_layer = call(edge_kernel, (volume,), (row, row, layer, layer), [], "edges")
    above = lax.ppermute(last_row, "by", up_y)
    below = lax.ppermute(first_row, "by", down_y)
    before = lax.ppermute(last_layer, "bx", up_x)
    after = lax.ppermute(first_layer, "bx", down_x)
    busy = pl.CostEstimate(flops=40 * layers * half * depth, bytes_accessed=2 * layers * rows * depth, transcendentals=0)
    part = call(
        functools.partial(inner_kernel, layers * size_x),
        (volume, view),
        shape((5, half, depth), F32),
        [field, field, sign],
        "inner",
        busy,
    )
    codes = call(
        functools.partial(outer_kernel, layers * size_x),
        (volume, before, after, above, below, view, part),
        shape((size_x, 4, half, LANES), jnp.int16),
        [field, field, sign, pltpu.VMEM((4, rows, depth), F32)],
        "outer",
        busy,
    )
    codes = lax.all_to_all(codes, "bx", split_axis=0, concat_axis=0, tiled=True)
    return call(fold_kernel, (codes, view), shape((4, rows, depth // size_x), F32), [], "fold")


def solution(mesh):
    placed = (P("bx", "by", None), P("by"))
    return jax.shard_map(body, mesh=mesh, in_specs=placed, out_specs=P(None, "by", "bx"), check_vma=False)
```

time: 52.9 us -> 46.4 us (0.88)
  blocking collectives: 0 us -> 20.5 us
  waiting for transfers between devices: 15 us -> 0.43 us
  starting transfers between devices: 21.4 us -> 12.4 us
  local copies, waits for them, and re-layouts: 4.36 us -> 1.59 us
  other arithmetic: 0.74 us -> 0 us
    all_to_all x0 -> x1, blocking collectives: none -> 20.5 us  [body(): codes = lax.all_to_all(codes, 'bx', split_axis=0, concat_axis=0, tiled=True)]
    all_to_all x1 -> x0, waiting for transfers between devices: 11.3 us -> none  [body(): codes = lax.all_to_all(codes, 'bx', split_axis=0, concat_axis=0, tiled=True)]
    all_to_all x1 -> x0, starting transfers between devices: 9.06 us -> none  [body(): codes = lax.all_to_all(codes, 'bx', split_axis=0, concat_axis=0, tiled=True)]
    ppermute x4, waiting for transfers between devices: 3.64 us -> 0.43 us  [the longest x1 0.42 us: body(): below = lax.ppermute(first_row, 'by', down_y)]
    slice x3 -> x0, local copies, waits for them, and re-layouts: 2.47 us -> none  [the longest x1 1.41 us: body(): below = lax.ppermute(volume[:, 0, :], 'by', down_y)]
    select_n x1 -> x0, other arithmetic: 0.66 us -> none  [body(): side = jnp.where(view_side == 1, 1.0, -1.0).astype(F32)]
    pallas_call x2 -> x4, Pallas kernels: 11 us -> 11.3 us  [call(): pl.pallas_call(kernel, out_shape=out_shape, in_specs=[in_vmem] * len(oper...]
  transfers between devices with their start and end apart: 5 -> 4, of which waited for: 2 -> 1; matrix products, arithmetic and copies ran while one was open for 5% -> 0% of each run, Pallas kernels for 0% -> 8%
where the time goes in v2:
time: 46.4 us; the launch traced here: 46.2 us
  blocking collectives  20.5 us (44%)
  starting transfers between devices  12.4 us (27%)
  Pallas kernels  11.3 us (24%)
  local copies, waits for them, and re-layouts  1.59 us (3%)
    all_to_all x1, blocking collectives, body(): codes = lax.all_to_all(codes, 'bx', split_axis=0, concat_axis=0, tiled=True)  20.5 us
    pallas_call x4, Pallas kernels, call(): pl.pallas_call(kernel, out_shape=out_shape, in_specs=[in_vmem] * len(oper...  11.3 us
    ppermute x1, starting transfers between devices, body(): above = lax.ppermute(last_row, 'by', up_y)  4.76 us
    ppermute x1, starting transfers between devices, body(): before = lax.ppermute(last_layer, 'bx', up_x)  3.77 us
    ppermute x1, starting transfers between devices, body(): after = lax.ppermute(first_layer, 'bx', down_x)  1.92 us
    ppermute x1, starting transfers between devices, body(): below = lax.ppermute(first_row, 'by', down_y)  1.92 us
    unnamed x4, local copies, waits for them, and re-layouts  1.59 us
  transfers between devices with their start and end apart: 4, of which 1 were waited for; matrix products, arithmetic and copies ran while one was open for 0% of the time, Pallas kernels for 8%

profile of v2, /device:TPU:225, one launch (start us, length us, event | category | flops | bytes accessed | tf_op | source)
XLA Modules:
  0.0 46.2 jit_solution(15108612431128314182)
XLA Ops:
  0.0 0.0 copy-start
  0.0 1.6 %copy-done = bf16[16,32,2048]{2,1,0:T(8,128)(2,1)S(1)} copy-done((bf16[16,32,2048]{2,1,0:T(8,128)(2,1)S(1)}, bf16[16,32,2048]{2,1,0:T(8,128)(2,1)}, u32[]{:S(2)}) %copy-start) | copy-done | bytes 2097176
  1.6 0.0 copy-start.1
  1.6 0.4 edges.1
  2.0 3.8 %collective-permute-start = (bf16[32,2048]{1,0:T(8,128)(2,1)S(1)}, bf16[32,2048]{1,0:T(8,128)(2,1)S(1)}, u32[]{:S(2)}, u32[]{:S(2)}) collective-permute-start(bf16[32,2048]{1,0:T(8,128)(2,1)S(1)} %get-tuple-element.9), channel_id=1, source_target_pairs={{0,16},{16,32},{32,48},{48,64},{64,80},{80,96},{96,112},{112,128},... | collective-permute-start | bytes 393224 | tf_op jit(solution)/shard_map/ppermute | solution.py:285
  5.7 1.9 %collective-permute-start.1 = (bf16[32,2048]{1,0:T(8,128)(2,1)S(1)}, bf16[32,2048]{1,0:T(8,128)(2,1)S(1)}, u32[]{:S(2)}, u32[]{:S(2)}) collective-permute-start(bf16[32,2048]{1,0:T(8,128)(2,1)S(1)} %get-tuple-element.10), channel_id=1, source_target_pairs={{16,0},{32,16},{48,32},{64,48},{80,64},{96,80},{112,96},{128,112},... | collective-permute-start | bytes 393224 | tf_op jit(solution)/shard_map/ppermute | solution.py:286
  7.7 4.8 %collective-permute-start.2 = (bf16[16,2048]{1,0:T(8,128)(2,1)S(1)}, bf16[16,2048]{1,0:T(8,128)(2,1)S(1)}, u32[]{:S(2)}, u32[]{:S(2)}) collective-permute-start(bf16[16,2048]{1,0:T(8,128)(2,1)S(1)} %get-tuple-element.11), channel_id=1, source_target_pairs={{0,1},{1,2},{2,3},{3,4},{4,5},{5,6},{6,7},{7,8},{8,9},{9,10},{10,1... | collective-permute-start | bytes 196616 | tf_op jit(solution)/shard_map/ppermute | solution.py:283
  12.4 1.9 %collective-permute-start.3 = (bf16[16,2048]{1,0:T(8,128)(2,1)S(1)}, bf16[16,2048]{1,0:T(8,128)(2,1)S(1)}, u32[]{:S(2)}, u32[]{:S(2)}) collective-permute-start(bf16[16,2048]{1,0:T(8,128)(2,1)S(1)} %get-tuple-element.12), channel_id=1, source_target_pairs={{1,0},{2,1},{3,2},{4,3},{5,4},{6,5},{7,6},{8,7},{9,8},{10,9},{11,1... | collective-permute-start | bytes 196616 | tf_op jit(solution)/shard_map/ppermute | solution.py:284
  14.3 0.0 copy-done.1
  14.4 3.8 %inner.1.part = f32[5,16,2048]{2,1,0:T(8,128)S(1)} custom-call(bf16[16,32,2048]{2,1,0:T(8,128)(2,1)S(1)} %copy-done, s32[1,32]{1,0:T(1,128)S(1)} %bitcast.1), custom_call_target="tpu_custom_call" | custom-call | flops 20971520 | bytes 2097152 | tf_op jit(solution)/shard_map/inner/pallas_call | solution.py:268
  18.2 0.0 collective-permute-done.2.above
  18.2 0.4 collective-permute-done.3.below
  18.6 0.0 collective-permute-done.before
  18.6 0.0 collective-permute-done.1.after
  18.6 6.0 %outer.1 = s16[32,4,16,128]{3,2,1,0:T(8,128)(2,1)S(1)} custom-call(bf16[16,32,2048]{2,1,0:T(8,128)(2,1)S(1)} %copy-done, bf16[32,2048]{1,0:T(8,128)(2,1)S(1)} %collective-permute-done.before, bf16[32,2048]{1,0:T(8,128)(2,1)S(1)} %collective-permute-done.1.after, bf16[16,2048]{1,0:T(8,128)(2,1)S(1)} %collective-permute-done.2.above, ...), custom_call_target="tpu_custom_call" | custom-call | flops 20971520 | bytes 2097152 | tf_op jit(solution)/shard_map/outer/pallas_call | solution.py:268
  24.7 20.5 %all_to_all.5.codes = s16[32,4,16,128]{3,2,1,0:T(8,128)(2,1)S(1)} all-to-all(s16[32,4,16,128]{3,2,1,0:T(8,128)(2,1)S(1)} %outer.1), channel_id=1, replica_groups=mesh['bx'=32,'by'=16] {'bx'}, dimensions={0} | all-to-all | bytes 1048576 | tf_op jit(solution)/shard_map/all_to_all | solution.py:304
  45.1 1.1 %fold.1 = f32[4,32,64]{2,1,0:T(8,128)} custom-call(s16[32,4,16,128]{3,2,1,0:T(8,128)(2,1)S(1)} %all_to_all.5.codes, s32[1,32]{1,0:T(1,128)S(1)} %bitcast.3), custom_call_target="tpu_custom_call" | custom-call | tf_op jit(solution)/shard_map/fold/pallas_call | solution.py:268
Async XLA Ops:
  0.0 1.6 %copy-start = (bf16[16,32,2048]{2,1,0:T(8,128)(2,1)S(1)}, bf16[16,32,2048]{2,1,0:T(8,128)(2,1)}, u32[]{:S(2)}) copy-start(bf16[16,32,2048]{2,1,0:T(8,128)(2,1)} %vol.5) | copy-start | bytes 6291460
  1.6 12.8 %copy-start.1 = (s32[32]{0:T(128)S(1)}, s32[32]{0:T(128)}, u32[]{:S(2)}) copy-start(s32[32]{0:T(128)} %param.3) | copy-start | bytes 388
  2.0 16.7 %collective-permute-start = (bf16[32,2048]{1,0:T(8,128)(2,1)S(1)}, bf16[32,2048]{1,0:T(8,128)(2,1)S(1)}, u32[]{:S(2)}, u32[]{:S(2)}) collective-permute-start(bf16[32,2048]{1,0:T(8,128)(2,1)S(1)} %get-tuple-element.9), channel_id=1, source_target_pairs={{0,16},{16,32},{32,48},{48,64},{64,80},{80,96},{96,112},{112,128},... | collective-permute-start | bytes 393224 | tf_op jit(solution)/shard_map/ppermute | solution.py:285
  5.7 12.9 %collective-permute-start.1 = (bf16[32,2048]{1,0:T(8,128)(2,1)S(1)}, bf16[32,2048]{1,0:T(8,128)(2,1)S(1)}, u32[]{:S(2)}, u32[]{:S(2)}) collective-permute-start(bf16[32,2048]{1,0:T(8,128)(2,1)S(1)} %get-tuple-element.10), channel_id=1, source_target_pairs={{16,0},{32,16},{48,32},{64,48},{80,64},{96,80},{112,96},{128,112},... | collective-permute-start | bytes 393224 | tf_op jit(solution)/shard_map/ppermute | solution.py:286
  7.7 10.6 %collective-permute-start.2 = (bf16[16,2048]{1,0:T(8,128)(2,1)S(1)}, bf16[16,2048]{1,0:T(8,128)(2,1)S(1)}, u32[]{:S(2)}, u32[]{:S(2)}) collective-permute-start(bf16[16,2048]{1,0:T(8,128)(2,1)S(1)} %get-tuple-element.11), channel_id=1, source_target_pairs={{0,1},{1,2},{2,3},{3,4},{4,5},{5,6},{6,7},{7,8},{8,9},{9,10},{10,1... | collective-permute-start | bytes 196616 | tf_op jit(solution)/shard_map/ppermute | solution.py:283
  12.4 6.2 %collective-permute-start.3 = (bf16[16,2048]{1,0:T(8,128)(2,1)S(1)}, bf16[16,2048]{1,0:T(8,128)(2,1)S(1)}, u32[]{:S(2)}, u32[]{:S(2)}) collective-permute-start(bf16[16,2048]{1,0:T(8,128)(2,1)S(1)} %get-tuple-element.12), channel_id=1, source_target_pairs={{1,0},{2,1},{3,2},{4,3},{5,4},{6,5},{7,6},{8,7},{9,8},{10,9},{11,1... | collective-permute-start | bytes 196616 | tf_op jit(solution)/shard_map/ppermute | solution.py:284

commit v3 on v2

v3 whole, which is shorter than its diff:
```python
import functools
import math

import jax
import jax.numpy as jnp
from jax import lax
from jax.experimental import pallas as pl
from jax.experimental.pallas import tpu as pltpu
from jax.sharding import PartitionSpec as P

F32 = jnp.float32
BF16 = jnp.bfloat16
LANES = 128
TILES = 8
LOG2E = 1.0 / math.log(2.0)
FLOOR = -27.0
STEPS = 2621.0
TONE = 0.7 * 0.48 * 0.48


def recip(x):
    return pl.reciprocal(x, approx=True)


def lane_tile(start):
    return pl.ds(pl.multiple_of(start, LANES), LANES)


def encode(value):
    level = jnp.log2(jnp.maximum(value, 2.0**FLOOR)) * STEPS + (0.5 - FLOOR * STEPS)
    return level.astype(jnp.int32) - 32768


def decode(code):
    code = code.astype(jnp.int32)
    value = jnp.exp2(code.astype(F32) * (1.0 / STEPS) + (32768.0 / STEPS + FLOOR))
    return jnp.where(code == -32768, 0.0, value)


def side_column(view):
    rows = view.shape[1]
    spread = jnp.broadcast_to(view[...].astype(F32), (rows, rows))
    down = lax.broadcasted_iota(jnp.int32, (rows, rows), 0)
    along = lax.broadcasted_iota(jnp.int32, (rows, rows), 1)
    picked = jnp.sum(jnp.where(down == along, spread, 0.0), axis=1, keepdims=True)
    return jnp.where(picked > 0.5, 1.0, -1.0)


def edge_kernel(vol, first_row, last_row, first_layer, last_layer):
    layers, rows, depth = vol.shape

    def tile(z, carry):
        here = lane_tile(LANES * z)
        first_row[:, here] = jnp.concatenate([vol[l, :, here].astype(F32)[:1] for l in range(layers)], 0).astype(BF16)
        last_row[:, here] = jnp.concatenate([vol[l, :, here].astype(F32)[rows - 1 :] for l in range(layers)], 0).astype(BF16)
        first_layer[:, here] = vol[0, :, here]
        last_layer[:, here] = vol[layers - 1, :, here]
        return carry

    lax.fori_loop(0, depth // LANES, tile, 0, unroll=2)


class March:
    def __init__(self, field, ray_length, group):
        self.field, self.group = field, group
        self.lane = lax.broadcasted_iota(jnp.int32, (8, LANES), 1)
        self.row = lax.broadcasted_iota(jnp.int32, (8, LANES), 0)

    def tile(self, t):
        return self.group * TILES + t

    def here(self, t):
        return lane_tile(LANES * self.tile(t))

    def at(self, l, t, row):
        return self.field[l, self.tile(t) + 1, pl.ds(row, 8), :]

    def fresh(self):
        return dict(
            path=[jnp.zeros((8, LANES), F32) for _ in range(TILES)],
            reach=[jnp.ones((8, LANES), F32) for _ in range(TILES)],
            color=[[jnp.zeros((8, LANES), F32) for _ in range(TILES)] for _ in range(4)],
        )

    def layer(self, r, l, rate, state, before=None, after=None, above=None, below=None):
        lane, r8 = self.lane, 8 * r
        path, reach, color = state["path"], state["reach"], state["color"]
        mid = [self.at(l, t, r8) for t in range(-1, TILES + 1)]
        from_left = [pltpu.roll(v, 1, 1) for v in mid[:-1]]
        from_right = [pltpu.roll(v, LANES - 1, 1) for v in mid[1:]]
        for t in range(TILES):
            v = mid[t + 1]
            if above is None:
                up = self.at(l, t, r8 - 1)
            else:
                up = jnp.where(self.row == 0, above[pl.ds(l, 1), self.here(t)], pltpu.roll(v, 1, 0))
            if below is None:
                down = self.at(l, t, r8 + 1)
            else:
                down = jnp.where(self.row == 7, below[pl.ds(l, 1), self.here(t)], pltpu.roll(v, 7, 0))
            back = self.at(l - 1, t, r8) if before is None else edge_rows(before, r, self.here(t))
            front = self.at(l + 1, t, r8) if after is None else edge_rows(after, r, self.here(t))
            gx = front - back
            gy = down - up
            gz = jnp.where(lane == LANES - 1, from_right[t + 1], from_right[t]) - jnp.where(
                lane == 0, from_left[t], from_left[t + 1]
            )
            square = gx * gx + gy * gy + gz * gz
            facing = gx + (0.6 / 0.48) * gy + (0.64 / 0.48) * gz
            shading = 0.3 / TONE + facing * facing * recip(square + 4.0)
            lifted = jnp.maximum(v, 0.4)
            density = jnp.minimum(lifted, 1.6) - 0.4
            path[t] = path[t] + density * (rate[0][...] - rate[1][...] * recip(square + 1.0))
            next_reach = jnp.exp2(path[t])
            weight = (next_reach - reach[t]) * shading
            reach[t] = next_reach
            color[0][t] = color[0][t] + weight * jnp.clip(v, 0.8, 1.8)
            color[1][t] = color[1][t] + weight * jnp.minimum(v, 2.0 - v)
            color[2][t] = color[2][t] + weight * jnp.minimum(lifted, 1.2)
            color[3][t] = color[3][t] + weight


def edge_rows(layer, r, here):
    return layer[pl.ds(16 * (r // 2), 16), here].astype(F32)[8 * (r % 2) : 8 * (r % 2) + 8]


def set_rates(view, ray_length, rates):
    rows = rates.shape[1]
    side = jnp.broadcast_to(side_column(view), (rows, LANES))
    scale = 3.0 / 1.2 / ray_length * LOG2E
    rates[0] = side * (1.25 * scale)
    rates[1] = side * scale


def rates_of(rates, r):
    return rates.at[0, pl.ds(8 * r, 8)], rates.at[1, pl.ds(8 * r, 8)]


def inner_kernel(ray_length, vol, view, part, field, rates):
    layers, rows, depth = vol.shape
    tiles = depth // LANES
    set_rates(view, ray_length, rates)

    def widen(l, carry):
        field[l, 0] = jnp.zeros((rows, LANES), F32)
        field[l, tiles + 1] = jnp.zeros((rows, LANES), F32)
        for tile in range(tiles):
            field[l, tile + 1] = vol[l, :, pl.ds(LANES * tile, LANES)].astype(F32)
        return carry

    lax.fori_loop(0, layers, widen, 0)

    def work(group, carry):
        march = March(field, ray_length, group)
        for r in (1, 2):
            state = march.fresh()
            for l in range(1, layers - 1):
                march.layer(r, l, rates_of(rates, r), state)
            for t in range(TILES):
                for k, kind in enumerate([state["path"]] + state["color"]):
                    part[k, pl.ds(8 * r - 8, 8), march.here(t)] = kind[t]
        return carry

    lax.fori_loop(0, tiles // TILES, work, 0)


def outer_kernel(ray_length, before, after, above, below, view, part, field, codes, rates, above_wide, below_wide, levels):
    layers, _, rows, _ = field.shape
    tiles = part.shape[2] // LANES
    set_rates(view, ray_length, rates)
    above_wide[...] = above[...].astype(F32)
    below_wide[...] = below[...].astype(F32)
    half = rows // 2

    def work(group, carry):
        march = March(field, ray_length, group)

        def finish(r, state):
            side = rates[1, pl.ds(8 * r, 8)]
            for t in range(TILES):
                path = state["path"][t]
                red, green, blue, total = (kind[t] for kind in state["color"])
                factor = jnp.where(side > 0, jnp.exp2(-path), -1.0) * TONE
                final = [(red - 0.8 * total) * factor, green * factor, (1.2 * total - blue) * factor, jnp.abs(path)]
                for k in range(4):
                    levels[k, t, pl.ds(8 * r, 8), :] = encode(final[k])

        for r in (0, 3):
            rate = rates_of(rates, r)
            state = march.fresh()
            for l in range(layers):
                march.layer(
                    r,
                    l,
                    rate,
                    state,
                    before if l == 0 else None,
                    after if l == layers - 1 else None,
                    above_wide if r == 0 else None,
                    below_wide if r == 3 else None,
                )
            finish(r, state)
        for r in (1, 2):
            rate = rates_of(rates, r)
            state = march.fresh()
            march.layer(r, 0, rate, state, before=before)
            for t in range(TILES):
                block = [part[k, pl.ds(8 * r - 8, 8), march.here(t)] for k in range(5)]
                for k in range(4):
                    state["color"][k][t] = state["color"][k][t] + state["reach"][t] * block[k + 1]
                state["path"][t] = state["path"][t] + block[0]
                state["reach"][t] = jnp.exp2(state["path"][t])
            march.layer(r, layers - 1, rate, state, after=after)
            finish(r, state)
        low = lax.broadcasted_iota(jnp.int32, (half, LANES), 1) < LANES // 2
        for t in range(TILES):
            z = march.tile(t)
            for k in range(4):
                top, bottom = levels[k, t, pl.ds(0, half)], levels[k, t, pl.ds(half, half)]
                codes[2 * z, k] = jnp.where(low, top, pltpu.roll(bottom, LANES // 2, 1)).astype(jnp.int16)
                codes[2 * z + 1, k] = jnp.where(low, pltpu.roll(top, LANES // 2, 1), bottom).astype(jnp.int16)
        return carry

    lax.fori_loop(0, tiles // TILES, work, 0)


def fold_kernel(codes, view, out):
    bricks, _, half, _ = codes.shape
    column = side_column(view)
    low = lax.broadcasted_iota(jnp.int32, (half, LANES), 1) < LANES // 2
    side = jnp.where(low, column[:half], column[half:])
    backward = side > 0
    path = jnp.zeros((half, LANES), F32)
    color = [jnp.zeros((half, LANES), F32) for _ in range(3)]
    for k in range(bricks):
        farther = path + decode(codes[k, 3])
        reach = jnp.exp2(side * jnp.where(backward, farther, path))
        path = farther
        for q in range(3):
            color[q] = color[q] + reach * decode(codes[k, q])
    passing = jnp.exp2(-path)
    factor = jnp.where(backward, passing, 1.0)
    parts = [c * factor for c in color] + [1.0 - passing]
    for q in range(4):
        out[q, pl.ds(0, half), :] = parts[q][:, : LANES // 2]
        out[q, pl.ds(half, half), :] = parts[q][:, LANES // 2 :]


def body(volume, view_side):
    layers, rows, depth = volume.shape
    size_x, size_y = lax.axis_size("bx"), lax.axis_size("by")
    up_x = [(i, i + 1) for i in range(size_x - 1)]
    up_y = [(i, i + 1) for i in range(size_y - 1)]
    down_x = [(j, i) for i, j in up_x]
    down_y = [(j, i) for i, j in up_y]
    view = view_side[None, :]
    half = rows // 2
    in_vmem = pl.BlockSpec(memory_space=pltpu.VMEM)
    shape = jax.ShapeDtypeStruct

    def call(kernel, operands, out_shape, scratch, name, cost=None, limit=24):
        return pl.pallas_call(
            kernel,
            out_shape=out_shape,
            in_specs=[in_vmem] * len(operands),
            out_specs=jax.tree.map(lambda _: in_vmem, out_shape),
            scratch_shapes=scratch,
            compiler_params=pltpu.CompilerParams(vmem_limit_bytes=limit << 20),
            cost_estimate=cost,
            name=name,
        )(*operands)

    rates = pltpu.VMEM((2, rows, LANES), F32)
    row, layer = shape((layers, depth), BF16), shape((rows, depth), BF16)
    first_row, last_row, first_layer, last_layer = call(edge_kernel, (volume,), (row, row, layer, layer), [], "edges")
    above = lax.ppermute(last_row, "by", up_y)
    below = lax.ppermute(first_row, "by", down_y)
    before = lax.ppermute(last_layer, "bx", up_x)
    after = lax.ppermute(first_layer, "bx", down_x)
    busy = pl.CostEstimate(flops=40 * layers * half * depth, bytes_accessed=2 * layers * rows * depth, transcendentals=0)
    part, field = call(
        functools.partial(inner_kernel, layers * size_x),
        (volume, view),
        (shape((5, half, depth), F32), shape((layers, depth // LANES + 2, rows, LANES), F32)),
        [rates],
        "inner",
        busy,
    )
    wide = pltpu.VMEM((layers, depth), F32)
    codes = call(
        functools.partial(outer_kernel, layers * size_x),
        (before, after, above, below, view, part, field),
        shape((size_x, 4, half, LANES), jnp.int16),
        [rates, wide, wide, pltpu.VMEM((4, TILES, rows, LANES), jnp.int32)],
        "outer",
        busy,
    )
    codes = lax.all_to_all(codes, "bx", split_axis=0, concat_axis=0, tiled=True)
    return call(fold_kernel, (codes, view), shape((4, rows, depth // size_x), F32), [], "fold")


def solution(mesh):
    placed = (P("bx", "by", None), P("by"))
    return jax.shard_map(body, mesh=mesh, in_specs=placed, out_specs=P(None, "by", "bx"), check_vma=False)
```

time: 46.4 us -> 44.9 us (0.968)
  Pallas kernels: 11.3 us -> 9.19 us
  local copies, waits for them, and re-layouts: 1.59 us -> 2.24 us
    pallas_call x4, Pallas kernels: 11.3 us -> 9.19 us  [call(): pl.pallas_call(kernel, out_shape=out_shape, in_specs=[in_vmem] * len(oper...]
    unnamed x4, local copies, waits for them, and re-layouts: 1.59 us -> 2.24 us
  transfers between devices with their start and end apart: 4 -> 4, of which waited for: 1 -> 1; matrix products, arithmetic and copies ran while one was open for 0% -> 0% of each run, Pallas kernels for 8% -> 7%
where the time goes in v3:
time: 44.9 us; the launch traced here: 44.7 us
  blocking collectives  20.5 us (46%)
  starting transfers between devices  12.4 us (28%)
  Pallas kernels  9.19 us (20%)
  local copies, waits for them, and re-layouts  2.24 us (5%)
    all_to_all x1, blocking collectives, body(): codes = lax.all_to_all(codes, 'bx', split_axis=0, concat_axis=0, tiled=True)  20.5 us
    pallas_call x4, Pallas kernels, call(): pl.pallas_call(kernel, out_shape=out_shape, in_specs=[in_vmem] * len(oper...  9.19 us
    ppermute x1, starting transfers between devices, body(): above = lax.ppermute(last_row, 'by', up_y)  4.76 us
    ppermute x1, starting transfers between devices, body(): before = lax.ppermute(last_layer, 'bx', up_x)  3.77 us
    unnamed x4, local copies, waits for them, and re-layouts  2.24 us
    ppermute x1, starting transfers between devices, body(): after = lax.ppermute(first_layer, 'bx', down_x)  1.92 us
    ppermute x1, starting transfers between devices, body(): below = lax.ppermute(first_row, 'by', down_y)  1.92 us
  transfers between devices with their start and end apart: 4, of which 1 were waited for; matrix products, arithmetic and copies ran while one was open for 0% of the time, Pallas kernels for 7%

profile of v3, /device:TPU:225, one launch (start us, length us, event | category | flops | bytes accessed | tf_op | source)
XLA Modules:
  0.0 44.7 jit_solution(13619179529617956641)
XLA Ops:
  0.0 0.0 copy-start
  0.0 1.6 %copy-done = bf16[16,32,2048]{2,1,0:T(8,128)(2,1)S(1)} copy-done((bf16[16,32,2048]{2,1,0:T(8,128)(2,1)S(1)}, bf16[16,32,2048]{2,1,0:T(8,128)(2,1)}, u32[]{:S(2)}) %copy-start) | copy-done | bytes 2097176
  1.6 0.4 edges.1
  2.0 3.8 %collective-permute-start = (bf16[32,2048]{1,0:T(8,128)(2,1)S(1)}, bf16[32,2048]{1,0:T(8,128)(2,1)S(1)}, u32[]{:S(2)}, u32[]{:S(2)}) collective-permute-start(bf16[32,2048]{1,0:T(8,128)(2,1)S(1)} %get-tuple-element.11), channel_id=1, source_target_pairs={{0,16},{16,32},{32,48},{48,64},{64,80},{80,96},{96,112},{112,128},... | collective-permute-start | bytes 393224 | tf_op jit(solution)/shard_map/ppermute | solution.py:278
  5.7 1.9 %collective-permute-start.1 = (bf16[32,2048]{1,0:T(8,128)(2,1)S(1)}, bf16[32,2048]{1,0:T(8,128)(2,1)S(1)}, u32[]{:S(2)}, u32[]{:S(2)}) collective-permute-start(bf16[32,2048]{1,0:T(8,128)(2,1)S(1)} %get-tuple-element.12), channel_id=1, source_target_pairs={{16,0},{32,16},{48,32},{64,48},{80,64},{96,80},{112,96},{128,112},... | collective-permute-start | bytes 393224 | tf_op jit(solution)/shard_map/ppermute | solution.py:279
  7.7 4.8 %collective-permute-start.2 = (bf16[16,2048]{1,0:T(8,128)(2,1)S(1)}, bf16[16,2048]{1,0:T(8,128)(2,1)S(1)}, u32[]{:S(2)}, u32[]{:S(2)}) collective-permute-start(bf16[16,2048]{1,0:T(8,128)(2,1)S(1)} %get-tuple-element.13), channel_id=1, source_target_pairs={{0,1},{1,2},{2,3},{3,4},{4,5},{5,6},{6,7},{7,8},{8,9},{9,10},{10,1... | collective-permute-start | bytes 196616 | tf_op jit(solution)/shard_map/ppermute | solution.py:276
  12.4 1.9 %collective-permute-start.3 = (bf16[16,2048]{1,0:T(8,128)(2,1)S(1)}, bf16[16,2048]{1,0:T(8,128)(2,1)S(1)}, u32[]{:S(2)}, u32[]{:S(2)}) collective-permute-start(bf16[16,2048]{1,0:T(8,128)(2,1)S(1)} %get-tuple-element.14), channel_id=1, source_target_pairs={{1,0},{2,1},{3,2},{4,3},{5,4},{6,5},{7,6},{8,7},{9,8},{10,9},{11,1... | collective-permute-start | bytes 196616 | tf_op jit(solution)/shard_map/ppermute | solution.py:277
  14.3 0.0 copy-start.1
  14.4 0.6 %copy-done.1 = s32[32]{0:T(128)S(1)} copy-done((s32[32]{0:T(128)S(1)}, s32[32]{0:T(128)}, u32[]{:S(2)}) %copy-start.1) | copy-done | bytes 152
  15.0 3.3 %inner.1 = (f32[5,16,2048]{2,1,0:T(8,128)S(1)}, f32[16,18,32,128]{3,2,1,0:T(8,128)S(1)}) custom-call(bf16[16,32,2048]{2,1,0:T(8,128)(2,1)S(1)} %copy-done, s32[1,32]{1,0:T(1,128)S(1)} %bitcast.1), custom_call_target="tpu_custom_call" | custom-call | flops 20971520 | bytes 2097152 | tf_op jit(solution)/shard_map/inner/pallas_call | solution.py:262
  18.3 0.0 collective-permute-done.2.above
  18.3 0.3 collective-permute-done.3.below
  18.6 0.0 collective-permute-done.before
  18.6 0.0 collective-permute-done.1.after
  18.6 4.5 %outer.1 = s16[32,4,16,128]{3,2,1,0:T(8,128)(2,1)S(1)} custom-call(bf16[32,2048]{1,0:T(8,128)(2,1)S(1)} %collective-permute-done.before, bf16[32,2048]{1,0:T(8,128)(2,1)S(1)} %collective-permute-done.1.after, bf16[16,2048]{1,0:T(8,128)(2,1)S(1)} %collective-permute-done.2.above, bf16[16,2048]{1,0:T(8,128)(2,1)S(1)} %collective-permute-done.3.below, ...), custom_call_target="tpu_custom_call" | custom-call | flops 20971520 | bytes 2097152 | tf_op jit(solution)/shard_map/outer/pallas_call | solution.py:262
  23.1 20.5 %all_to_all.5.codes = s16[32,4,16,128]{3,2,1,0:T(8,128)(2,1)S(1)} all-to-all(s16[32,4,16,128]{3,2,1,0:T(8,128)(2,1)S(1)} %outer.1), channel_id=1, replica_groups=mesh['bx'=32,'by'=16] {'bx'}, dimensions={0} | all-to-all | bytes 1048576 | tf_op jit(solution)/shard_map/all_to_all | solution.py:298
  43.6 1.1 %fold.1 = f32[4,32,64]{2,1,0:T(8,128)} custom-call(s16[32,4,16,128]{3,2,1,0:T(8,128)(2,1)S(1)} %all_to_all.5.codes, s32[1,32]{1,0:T(1,128)S(1)} %bitcast.3), custom_call_target="tpu_custom_call" | custom-call | tf_op jit(solution)/shard_map/fold/pallas_call | solution.py:262
Async XLA Ops:
  0.0 1.6 %copy-start = (bf16[16,32,2048]{2,1,0:T(8,128)(2,1)S(1)}, bf16[16,32,2048]{2,1,0:T(8,128)(2,1)}, u32[]{:S(2)}) copy-start(bf16[16,32,2048]{2,1,0:T(8,128)(2,1)} %vol.3) | copy-start | bytes 6291460
  2.0 16.7 %collective-permute-start = (bf16[32,2048]{1,0:T(8,128)(2,1)S(1)}, bf16[32,2048]{1,0:T(8,128)(2,1)S(1)}, u32[]{:S(2)}, u32[]{:S(2)}) collective-permute-start(bf16[32,2048]{1,0:T(8,128)(2,1)S(1)} %get-tuple-element.11), channel_id=1, source_target_pairs={{0,16},{16,32},{32,48},{48,64},{64,80},{80,96},{96,112},{112,128},... | collective-permute-start | bytes 393224 | tf_op jit(solution)/shard_map/ppermute | solution.py:278
  5.7 12.9 %collective-permute-start.1 = (bf16[32,2048]{1,0:T(8,128)(2,1)S(1)}, bf16[32,2048]{1,0:T(8,128)(2,1)S(1)}, u32[]{:S(2)}, u32[]{:S(2)}) collective-permute-start(bf16[32,2048]{1,0:T(8,128)(2,1)S(1)} %get-tuple-element.12), channel_id=1, source_target_pairs={{16,0},{32,16},{48,32},{64,48},{80,64},{96,80},{112,96},{128,112},... | collective-permute-start | bytes 393224 | tf_op jit(solution)/shard_map/ppermute | solution.py:279
  7.7 10.6 %collective-permute-start.2 = (bf16[16,2048]{1,0:T(8,128)(2,1)S(1)}, bf16[16,2048]{1,0:T(8,128)(2,1)S(1)}, u32[]{:S(2)}, u32[]{:S(2)}) collective-permute-start(bf16[16,2048]{1,0:T(8,128)(2,1)S(1)} %get-tuple-element.13), channel_id=1, source_target_pairs={{0,1},{1,2},{2,3},{3,4},{4,5},{5,6},{6,7},{7,8},{8,9},{9,10},{10,1... | collective-permute-start | bytes 196616 | tf_op jit(solution)/shard_map/ppermute | solution.py:276
  12.4 6.2 %collective-permute-start.3 = (bf16[16,2048]{1,0:T(8,128)(2,1)S(1)}, bf16[16,2048]{1,0:T(8,128)(2,1)S(1)}, u32[]{:S(2)}, u32[]{:S(2)}) collective-permute-start(bf16[16,2048]{1,0:T(8,128)(2,1)S(1)} %get-tuple-element.14), channel_id=1, source_target_pairs={{1,0},{2,1},{3,2},{4,3},{5,4},{6,5},{7,6},{8,7},{9,8},{10,9},{11,1... | collective-permute-start | bytes 196616 | tf_op jit(solution)/shard_map/ppermute | solution.py:277
  14.3 0.7 %copy-start.1 = (s32[32]{0:T(128)S(1)}, s32[32]{0:T(128)}, u32[]{:S(2)}) copy-start(s32[32]{0:T(128)} %param.3) | copy-start | bytes 388

commit v4 on v3

v4 whole, which is shorter than its diff:
```python
import functools
import math

import jax
import jax.numpy as jnp
from jax import lax
from jax.experimental import pallas as pl
from jax.experimental.pallas import tpu as pltpu
from jax.sharding import PartitionSpec as P

F32 = jnp.float32
BF16 = jnp.bfloat16
LANES = 128
TILES = 8
LOG2E = 1.0 / math.log(2.0)
FLOOR = -27.0
STEPS = 2570.0
TONE = 0.7 * 0.48 * 0.48


def recip(x):
    return pl.reciprocal(x, approx=True)


def lane_tile(start):
    return pl.ds(pl.multiple_of(start, LANES), LANES)


def encode(value):
    level = jnp.log2(jnp.maximum(value, 2.0**FLOOR)) * STEPS + (0.5 - FLOOR * STEPS)
    return level.astype(jnp.int32) - 32768


def decode(code):
    code = code.astype(jnp.int32)
    value = jnp.exp2(code.astype(F32) * (1.0 / STEPS) + (32768.0 / STEPS + FLOOR))
    return jnp.where(code == -32768, 0.0, value)


def core_index():
    return lax.rem(lax.axis_index("bx"), 2)


def side_column(view):
    rows = view.shape[1]
    spread = jnp.broadcast_to(view[...].astype(F32), (rows, rows))
    down = lax.broadcasted_iota(jnp.int32, (rows, rows), 0)
    along = lax.broadcasted_iota(jnp.int32, (rows, rows), 1)
    picked = jnp.sum(jnp.where(down == along, spread, 0.0), axis=1, keepdims=True)
    return jnp.where(picked > 0.5, 1.0, -1.0)


def one_row(ref, row, here):
    return jnp.concatenate([ref[l, :, here].astype(F32)[row : row + 1] for l in range(16)], 0).astype(BF16)


def share_kernel(vol, send, keep):
    layers, rows, depth = vol.shape
    half = rows // 2

    def share(far, sent_row, kept_row):
        def tile(z, carry):
            here = lane_tile(LANES * z)
            for l in range(layers):
                send[l, :, here] = vol[l, pl.ds(far, half), here]
            send[layers, :, here] = one_row(vol, sent_row, here)
            keep[:, here] = one_row(vol, kept_row, here)
            return carry

        lax.fori_loop(0, depth // LANES, tile, 0, unroll=2)

    core = core_index()

    @pl.when(core == 0)
    def _():
        share(half, half - 1, half)

    @pl.when(core == 1)
    def _():
        share(0, half, half - 1)


def face_kernel(vol, mate, own, first, last, rim):
    layers, rows, depth = vol.shape
    half = rows // 2
    core = core_index()

    @pl.when(core == 0)
    def _():
        def tile(z, carry):
            here = lane_tile(LANES * z)
            first[:, here] = vol[0, pl.ds(0, half), here]
            last[:, here] = mate[layers - 1, :, here]
            rim[pl.ds(0, layers), here] = one_row(vol, 0, here)
            rim[pl.ds(layers, layers), here] = one_row(mate, 0, here)
            return carry

        lax.fori_loop(0, depth // LANES, tile, 0, unroll=2)

    @pl.when(core == 1)
    def _():
        def tile(z, carry):
            here = lane_tile(LANES * z)
            first[:, here] = mate[0, :, here]
            last[:, here] = vol[layers - 1, pl.ds(half, half), here]
            rim[pl.ds(0, layers), here] = one_row(mate, half - 1, here)
            rim[pl.ds(layers, layers), here] = one_row(vol, rows - 1, here)
            return carry

        lax.fori_loop(0, depth // LANES, tile, 0, unroll=2)


class March:
    def __init__(self, field, group):
        self.field, self.group = field, group
        self.lane = lax.broadcasted_iota(jnp.int32, (8, LANES), 1)

    def tile(self, t):
        return self.group * TILES + t

    def here(self, t):
        return lane_tile(LANES * self.tile(t))

    def at(self, l, t, row):
        return self.field[l, self.tile(t) + 1, pl.ds(row, 8), :]

    def fresh(self):
        return dict(
            path=[jnp.zeros((8, LANES), F32) for _ in range(TILES)],
            reach=[jnp.ones((8, LANES), F32) for _ in range(TILES)],
            color=[[jnp.zeros((8, LANES), F32) for _ in range(TILES)] for _ in range(4)],
        )

    def layer(self, row, l, rate, state, before=None, after=None, rim=None):
        lane = self.lane
        path, reach, color = state["path"], state["reach"], state["color"]
        mid = [self.at(l, t, row) for t in range(-1, TILES + 1)]
        from_left = [pltpu.roll(v, 1, 1) for v in mid[:-1]]
        from_right = [pltpu.roll(v, LANES - 1, 1) for v in mid[1:]]
        for t in range(TILES):
            v = mid[t + 1]
            up, down = self.at(l, t, row - 1), self.at(l, t, row + 1)
            if rim is not None:
                beyond = jnp.broadcast_to(rim[0][pl.ds(l, 1), self.here(t)], (8, LANES))
                up, down = jnp.where(rim[1], beyond, up), jnp.where(rim[2], beyond, down)
            back = self.at(l - 1, t, row) if before is None else before[:, self.here(t)]
            front = self.at(l + 1, t, row) if after is None else after[:, self.here(t)]
            gx = front - back
            gy = down - up
            gz = jnp.where(lane == LANES - 1, from_right[t + 1], from_right[t]) - jnp.where(
                lane == 0, from_left[t], from_left[t + 1]
            )
            square = gx * gx + gy * gy + gz * gz
            facing = gx + (0.6 / 0.48) * gy + (0.64 / 0.48) * gz
            shading = 0.3 / TONE + facing * facing * recip(square + 4.0)
            lifted = jnp.maximum(v, 0.4)
            density = jnp.minimum(lifted, 1.6) - 0.4
            path[t] = path[t] + density * (rate[0][...] - rate[1][...] * recip(square + 1.0))
            next_reach = jnp.exp2(path[t])
            weight = (next_reach - reach[t]) * shading
            reach[t] = next_reach
            color[0][t] = color[0][t] + weight * jnp.clip(v, 0.8, 1.8)
            color[1][t] = color[1][t] + weight * jnp.minimum(v, 2.0 - v)
            color[2][t] = color[2][t] + weight * jnp.minimum(lifted, 1.2)
            color[3][t] = color[3][t] + weight

    def keep(self, state, part):
        for t in range(TILES):
            for k, kind in enumerate([state["path"]] + state["color"]):
                part[k, :, self.here(t)] = kind[t]


def set_rates(view, ray_length, rates):
    rows = rates.shape[1]
    side = jnp.broadcast_to(side_column(view), (rows, LANES))
    scale = 3.0 / 1.2 / ray_length * LOG2E
    rates[0] = side * (1.25 * scale)
    rates[1] = side * scale


def rates_of(rates, row):
    here = pl.ds(pl.multiple_of(row, 8), 8)
    return rates.at[0, here], rates.at[1, here]


def own_kernel(ray_length, vol, view, part, field, rates):
    layers, rows, depth = vol.shape
    tiles = depth // LANES
    set_rates(view, ray_length, rates)

    def widen(l, carry):
        field[l, 0] = jnp.zeros((rows, LANES), F32)
        field[l, tiles + 1] = jnp.zeros((rows, LANES), F32)
        for tile in range(tiles):
            field[l, tile + 1] = vol[l, :, pl.ds(LANES * tile, LANES)].astype(F32)
        return carry

    lax.fori_loop(0, layers, widen, 0)
    row = pl.multiple_of(8 + 8 * core_index(), 8)

    def work(group, carry):
        march = March(field, group)
        state = march.fresh()
        for l in range(1, layers - 1):
            march.layer(row, l, rates_of(rates, row), state)
        march.keep(state, part)
        return carry

    lax.fori_loop(0, tiles // TILES, work, 0)


def mate_kernel(ray_length, vol, mate, keep, view, part, field, rates):
    layers, rows, depth = vol.shape
    tiles, half = depth // LANES, rows // 2
    set_rates(view, ray_length, rates)
    core = core_index()
    inside = pl.ds(8, half)
    mine, other = layers * core, layers * (1 - core)
    own_rows = pl.ds(pl.multiple_of(half * core, half), half)

    def widen(l, carry):
        for index in (mine + l, other + l):
            field[index, 0, inside, :] = jnp.zeros((half, LANES), F32)
            field[index, tiles + 1, inside, :] = jnp.zeros((half, LANES), F32)
        for tile in range(tiles):
            here = pl.ds(LANES * tile, LANES)
            field[mine + l, tile + 1, inside, :] = vol[l, own_rows, here].astype(F32)
            field[other + l, tile + 1, inside, :] = mate[l, :, here].astype(F32)
        return carry

    lax.fori_loop(0, layers, widen, 0)

    def border(slot, mine, other):
        def tile(z, carry):
            here = lane_tile(LANES * z)
            field[pl.ds(mine, layers), z + 1, slot, :] = keep[:, here].astype(F32)
            field[pl.ds(other, layers), z + 1, slot, :] = mate[layers, :, here].astype(F32)
            return carry

        lax.fori_loop(0, tiles, tile, 0, unroll=2)

    @pl.when(core == 0)
    def _():
        border(half + 8, 0, layers)

    @pl.when(core == 1)
    def _():
        border(7, layers, 0)

    row = pl.multiple_of(16 - 8 * core, 8)
    begin = layers - 1 - (layers - 2) * core

    def work(group, carry):
        march = March(field, group)
        state = march.fresh()
        for k in range(layers):
            march.layer(row, begin + k, rates_of(rates, 8 + 8 * core), state)
        march.keep(state, part)
        return carry

    lax.fori_loop(0, tiles // TILES, work, 0)


def rim_masks(core):
    rows_down = lax.broadcasted_iota(jnp.int32, (8, LANES), 0)
    return rows_down == 8 * core, rows_down == 8 - core


def rim_kernel(ray_length, beyond, view, field, part, rates, beyond_wide):
    layers = field.shape[0]
    tiles = part.shape[2] // LANES
    set_rates(view, ray_length, rates)
    beyond_wide[...] = beyond[...].astype(F32)
    core = core_index()
    above, below = rim_masks(core)
    row = pl.multiple_of(8 + 8 * core, 8)

    def work(group, carry):
        march = March(field, group)
        state = march.fresh()
        for l in range(1, layers - 1):
            march.layer(row, l, rates_of(rates, 24 * core), state, rim=(beyond_wide, above, below))
        march.keep(state, part)
        return carry

    lax.fori_loop(0, tiles // TILES, work, 0)


def outer_kernel(ray_length, before, after, beyond, view, own, other, border, field, codes, rates, before_wide, after_wide, beyond_wide, levels):
    layers = field.shape[0]
    tiles = own.shape[2] // LANES
    set_rates(view, ray_length, rates)
    before_wide[...] = before[...].astype(F32)
    after_wide[...] = after[...].astype(F32)
    beyond_wide[...] = beyond[...].astype(F32)
    core = core_index()
    above, below = rim_masks(core)
    own_first = jnp.zeros((8, LANES), jnp.int32) + core == 0
    low = lax.broadcasted_iota(jnp.int32, (8, LANES), 1) < LANES // 2

    def work(group, carry):
        march = March(field, group)

        def column(place, rate, blocks, rim):
            place = pl.multiple_of(place, 8)
            row = pl.multiple_of(8 + place, 8)
            state = march.fresh()
            march.layer(row, 0, rate, state, before=before_wide.at[pl.ds(place, 8)], rim=rim)
            for t in range(TILES):
                for block in blocks(t):
                    for k in range(4):
                        state["color"][k][t] = state["color"][k][t] + state["reach"][t] * block[k + 1]
                    state["path"][t] = state["path"][t] + block[0]
                    state["reach"][t] = jnp.exp2(state["path"][t])
            march.layer(row, layers - 1, rate, state, after=after_wide.at[pl.ds(place, 8)], rim=rim)
            side = rate[1][...]
            for t in range(TILES):
                path = state["path"][t]
                red, green, blue, total = (kind[t] for kind in state["color"])
                factor = jnp.where(side > 0, jnp.exp2(-path), -1.0) * TONE
                final = [(red - 0.8 * total) * factor, green * factor, (1.2 * total - blue) * factor, jnp.abs(path)]
                for k in range(4):
                    levels[k, t, pl.ds(place, 8), :] = encode(final[k])

        def outside(t):
            return [[border[k, :, march.here(t)] for k in range(5)]]

        def inside(t):
            mine = [own[k, :, march.here(t)] for k in range(5)]
            others = [other[k, :, march.here(t)] for k in range(5)]
            return (
                [jnp.where(own_first, a, b) for a, b in zip(mine, others)],
                [jnp.where(own_first, b, a) for a, b in zip(mine, others)],
            )

        column(8 * core, rates_of(rates, 24 * core), outside, (beyond_wide, above, below))
        column(8 - 8 * core, rates_of(rates, 8 + 8 * core), inside, None)
        for t in range(TILES):
            z = march.tile(t)
            even, odd = [], []
            for k in range(4):
                top, bottom = levels[k, t, pl.ds(0, 8)], levels[k, t, pl.ds(8, 8)]
                even.append(jnp.where(low, top, pltpu.roll(bottom, LANES // 2, 1)))
                odd.append(jnp.where(low, pltpu.roll(top, LANES // 2, 1), bottom))
            for k in range(2):
                codes[2 * z, k] = jnp.concatenate(even[2 * k : 2 * k + 2], 0).astype(jnp.int16)
                codes[2 * z + 1, k] = jnp.concatenate(odd[2 * k : 2 * k + 2], 0).astype(jnp.int16)
        return carry

    lax.fori_loop(0, tiles // TILES, work, 0)


def fold_kernel(codes, view, out):
    bricks = codes.shape[0]
    column = side_column(view)
    low = lax.broadcasted_iota(jnp.int32, (8, LANES), 1) < LANES // 2
    for core in range(2):
        base = 16 * core
        side = jnp.where(low, column[base : base + 8], column[base + 8 : base + 16])
        backward = side > 0
        path = jnp.zeros((8, LANES), F32)
        color = [jnp.zeros((8, LANES), F32) for _ in range(3)]
        for k in range(core, bricks, 2):
            values = [decode(codes[k, 0]), decode(codes[k, 1])]
            farther = path + values[1][8:]
            reach = jnp.exp2(side * jnp.where(backward, farther, path))
            path = farther
            color[0] = color[0] + reach * values[0][:8]
            color[1] = color[1] + reach * values[0][8:]
            color[2] = color[2] + reach * values[1][:8]
        passing = jnp.exp2(-path)
        factor = jnp.where(backward, passing, 1.0)
        parts = [c * factor for c in color] + [1.0 - passing]
        for q in range(4):
            out[q, pl.ds(base, 8), :] = parts[q][:, : LANES // 2]
            out[q, pl.ds(base + 8, 8), :] = parts[q][:, LANES // 2 :]


def body(volume, view_side):
    layers, rows, depth = volume.shape
    size_x, size_y = lax.axis_size("bx"), lax.axis_size("by")
    half = rows // 2
    mates = [(i, i ^ 1) for i in range(size_x)]
    up_x = [(i, i + 2) for i in range(size_x - 2)]
    down_x = [(j, i) for i, j in up_x]
    across = []
    for i in range(0, size_x, 2):
        for j in range(size_y - 1):
            upper, lower = (i + 1) * size_y + j, i * size_y + j + 1
            across += [(upper, lower), (lower, upper)]
    view = view_side[None, :]
    in_vmem = pl.BlockSpec(memory_space=pltpu.VMEM)
    shape = jax.ShapeDtypeStruct

    def call(kernel, operands, out_shape, scratch, name, cost=0, limit=24):
        return pl.pallas_call(
            kernel,
            out_shape=out_shape,
            in_specs=[in_vmem] * len(operands),
            out_specs=jax.tree.map(lambda _: in_vmem, out_shape),
            scratch_shapes=scratch,
            compiler_params=pltpu.CompilerParams(vmem_limit_bytes=limit << 20),
            cost_estimate=pl.CostEstimate(flops=cost, bytes_accessed=2 * layers * rows * depth, transcendentals=0) if cost else None,
            name=name,
        )(*operands)

    work = 40 * layers * half * depth
    length = layers * size_x
    rates = pltpu.VMEM((2, rows, LANES), F32)
    face, part = shape((half, depth), BF16), shape((5, 8, depth), F32)
    send, keep = call(share_kernel, (volume,), (shape((layers + 1, half, depth), BF16), face), [], "share")
    mate = lax.ppermute(send, "bx", mates)
    own = call(
        functools.partial(own_kernel, length),
        (volume, view),
        part,
        [pltpu.VMEM((layers, depth // LANES + 2, rows, LANES), F32), rates],
        "own",
        work // 2,
    )
    first, last, rim = call(face_kernel, (volume, mate, own), (face, face, shape((2 * layers, depth), BF16)), [], "face")
    beyond = lax.ppermute(rim, ("bx", "by"), across)
    before = lax.ppermute(last, "bx", up_x)
    after = lax.ppermute(first, "bx", down_x)
    other, field = call(
        functools.partial(mate_kernel, length),
        (volume, mate, keep, view),
        (part, shape((2 * layers, depth // LANES + 2, half + 16, LANES), F32)),
        [rates],
        "mate",
        work // 2,
    )
    wide, rim_wide = pltpu.VMEM((half, depth), F32), pltpu.VMEM((2 * layers, depth), F32)
    border = call(functools.partial(rim_kernel, length), (beyond, view, field), part, [rates, rim_wide], "rim", work)
    codes = call(
        functools.partial(outer_kernel, length),
        (before, after, beyond, view, own, other, border, field),
        shape((size_x, 2, 16, LANES), jnp.int16),
        [rates, wide, wide, rim_wide, pltpu.VMEM((4, TILES, 16, LANES), jnp.int32)],
        "outer",
        work,
    )
    codes = lax.all_to_all(codes, "bx", split_axis=0, concat_axis=0, tiled=True)
    return call(fold_kernel, (codes, view), shape((4, rows, depth // size_x), F32), [], "fold")


def solution(mesh):
    placed = (P("bx", "by", None), P("by"))
    return jax.shard_map(body, mesh=mesh, in_specs=placed, out_specs=P(None, "by", "bx"), check_vma=False)
```

time: 44.9 us -> 42.1 us (0.938)
  blocking collectives: 20.5 us -> 16.8 us
  Pallas kernels: 9.19 us -> 10.9 us
  local copies, waits for them, and re-layouts: 2.24 us -> 1.59 us
    all_to_all x1, blocking collectives: 20.5 us -> 16.8 us  [body(): codes = lax.all_to_all(codes, 'bx', split_axis=0, concat_axis=0, tiled=True)]
    pallas_call x4 -> x7, Pallas kernels: 9.19 us -> 10.9 us  [call(): pl.pallas_call(kernel, out_shape=out_shape, in_specs=[in_vmem] * len(oper...]
    unnamed x4, local copies, waits for them, and re-layouts: 2.24 us -> 1.59 us
  transfers between devices with their start and end apart: 4 -> 4, of which waited for: 1 -> 1; matrix products, arithmetic and copies ran while one was open for 0% -> 0% of each run, Pallas kernels for 7% -> 19%
where the time goes in v4:
time: 42.1 us; the launch traced here: 41.8 us
  blocking collectives  16.8 us (40%)
  starting transfers between devices  12.1 us (29%)
  Pallas kernels  10.9 us (26%)
  local copies, waits for them, and re-layouts  1.59 us (4%)
    all_to_all x1, blocking collectives, body(): codes = lax.all_to_all(codes, 'bx', split_axis=0, concat_axis=0, tiled=True)  16.8 us
    pallas_call x7, Pallas kernels, call(): pl.pallas_call(kernel, out_shape=out_shape, in_specs=[in_vmem] * len(oper...  10.9 us
    ppermute x1, starting transfers between devices, body(): beyond = lax.ppermute(rim, ('bx', 'by'), across)  5.02 us
    ppermute x1, starting transfers between devices, body(): before = lax.ppermute(last, 'bx', up_x)  3.2 us
    ppermute x1, starting transfers between devices, body(): mate = lax.ppermute(send, 'bx', mates)  2.58 us
    unnamed x4, local copies, waits for them, and re-layouts  1.59 us
    ppermute x1, starting transfers between devices, body(): after = lax.ppermute(first, 'bx', down_x)  1.29 us
  transfers between devices with their start and end apart: 4, of which 1 were waited for; matrix products, arithmetic and copies ran while one was open for 0% of the time, Pallas kernels for 19%

profile of v4, /device:TPU:225, one launch (start us, length us, event | category | flops | bytes accessed | tf_op | source)
XLA Modules:
  0.0 41.8 jit_solution(5456926845135591299)
XLA Ops:
  0.0 0.0 copy-start
  0.0 1.6 %copy-done = bf16[16,32,2048]{2,1,0:T(8,128)(2,1)S(1)} copy-done((bf16[16,32,2048]{2,1,0:T(8,128)(2,1)S(1)}, bf16[16,32,2048]{2,1,0:T(8,128)(2,1)}, u32[]{:S(2)}) %copy-start) | copy-done | bytes 2097176
  1.6 0.0 copy-start.1
  1.6 0.7 %share.1 = (bf16[17,16,2048]{2,1,0:T(8,128)(2,1)S(1)}, bf16[16,2048]{1,0:T(8,128)(2,1)S(1)}) custom-call(bf16[16,32,2048]{2,1,0:T(8,128)(2,1)S(1)} %copy-done), custom_call_target="tpu_custom_call" | custom-call | tf_op jit(solution)/shard_map/share/pallas_call | solution.py:396
  2.3 2.6 %collective-permute-start = (bf16[17,16,2048]{2,1,0:T(8,128)(2,1)S(1)}, bf16[17,16,2048]{2,1,0:T(8,128)(2,1)S(1)}, u32[]{:S(2)}, u32[]{:S(2)}) collective-permute-start(bf16[17,16,2048]{2,1,0:T(8,128)(2,1)S(1)} %get-tuple-element.12), channel_id=1, source_target_pairs={{0,16},{16,0},{32,48},{48,32},{64,80},{80,64},{96,112},{112,96},{1... | collective-permute-start | bytes 3342344 | tf_op jit(solution)/shard_map/ppermute | solution.py:412
  4.8 0.0 copy-done.1
  4.9 2.0 %own.1 = f32[5,8,2048]{2,1,0:T(8,128)S(1)} custom-call(bf16[16,32,2048]{2,1,0:T(8,128)(2,1)S(1)} %copy-done, s32[1,32]{1,0:T(1,128)S(1)} %bitcast.1), custom_call_target="tpu_custom_call" | custom-call | flops 10485760 | bytes 2097152 | tf_op jit(solution)/shard_map/own/pallas_call | solution.py:396
  6.8 0.4 collective-permute-done.mate
  7.2 0.3 face.1
  7.5 5.0 %collective-permute-start.3 = (bf16[32,2048]{1,0:T(8,128)(2,1)S(1)}, bf16[32,2048]{1,0:T(8,128)(2,1)S(1)}, u32[]{:S(2)}, u32[]{:S(2)}) collective-permute-start(bf16[32,2048]{1,0:T(8,128)(2,1)S(1)} %get-tuple-element.15), channel_id=1, source_target_pairs={{16,1},{1,16},{17,2},{2,17},{18,3},{3,18},{19,4},{4,19},{20,5},{5,... | collective-permute-start | bytes 393224 | tf_op jit(solution)/shard_map/ppermute | solution.py:422
  12.6 3.2 %collective-permute-start.1 = (bf16[16,2048]{1,0:T(8,128)(2,1)S(1)}, bf16[16,2048]{1,0:T(8,128)(2,1)S(1)}, u32[]{:S(2)}, u32[]{:S(2)}) collective-permute-start(bf16[16,2048]{1,0:T(8,128)(2,1)S(1)} %get-tuple-element.13), channel_id=1, source_target_pairs={{0,32},{16,48},{32,64},{48,80},{64,96},{80,112},{96,128},{112,144}... | collective-permute-start | bytes 196616 | tf_op jit(solution)/shard_map/ppermute | solution.py:423
  15.8 1.3 %collective-permute-start.2 = (bf16[16,2048]{1,0:T(8,128)(2,1)S(1)}, bf16[16,2048]{1,0:T(8,128)(2,1)S(1)}, u32[]{:S(2)}, u32[]{:S(2)}) collective-permute-start(bf16[16,2048]{1,0:T(8,128)(2,1)S(1)} %get-tuple-element.14), channel_id=1, source_target_pairs={{32,0},{48,16},{64,32},{80,48},{96,64},{112,80},{128,96},{144,112}... | collective-permute-start | bytes 196616 | tf_op jit(solution)/shard_map/ppermute | solution.py:424
  17.1 2.5 %mate.1 = (f32[5,8,2048]{2,1,0:T(8,128)S(1)}, f32[32,18,32,128]{3,2,1,0:T(8,128)S(1)}) custom-call(bf16[16,32,2048]{2,1,0:T(8,128)(2,1)S(1)} %copy-done, bf16[17,16,2048]{2,1,0:T(8,128)(2,1)S(1)} %collective-permute-done.mate, bf16[16,2048]{1,0:T(8,128)(2,1)S(1)} %get-tuple-element.16.keep, s32[1,32]{1,0:T(1,128)S(1)} %bitcast.2), custom_call_target="tpu_custom_call" | custom-call | flops 10485760 | bytes 2097152 | tf_op jit(solution)/shard_map/mate/pallas_call | solution.py:396
  19.6 0.0 collective-permute-done.3.beyond
  19.6 3.4 %rim.1.border = f32[5,8,2048]{2,1,0:T(8,128)S(1)} custom-call(bf16[32,2048]{1,0:T(8,128)(2,1)S(1)} %collective-permute-done.3.beyond, s32[1,32]{1,0:T(1,128)S(1)} %bitcast.3, f32[32,18,32,128]{3,2,1,0:T(8,128)S(1)} %get-tuple-element.18.field), custom_call_target="tpu_custom_call" | custom-call | flops 20971520 | bytes 2097152 | tf_op jit(solution)/shard_map/rim/pallas_call | solution.py:396
  23.0 0.0 collective-permute-done.1.before
  23.0 0.0 collective-permute-done.2.after
  23.0 1.1 %outer.1 = s16[32,2,16,128]{3,2,1,0:T(8,128)(2,1)S(1)} custom-call(bf16[16,2048]{1,0:T(8,128)(2,1)S(1)} %collective-permute-done.1.before, bf16[16,2048]{1,0:T(8,128)(2,1)S(1)} %collective-permute-done.2.after, bf16[32,2048]{1,0:T(8,128)(2,1)S(1)} %collective-permute-done.3.beyond, s32[1,32]{1,0:T(1,128)S(1)} %bitcast.4, f32[5,8,2048]{2,1,0:T(8,128)S(1)} %own.1, ...), custom_call_target="tpu_custom_call" | custom-call | flops 20971520 | bytes 2097152 | tf_op jit(solution)/shard_map/outer/pallas_call | solution.py:396
  24.2 16.8 %all_to_all.5.codes = s16[32,2,16,128]{3,2,1,0:T(8,128)(2,1)S(1)} all-to-all(s16[32,2,16,128]{3,2,1,0:T(8,128)(2,1)S(1)} %outer.1), channel_id=1, replica_groups=mesh['bx'=32,'by'=16] {'bx'}, dimensions={0} | all-to-all | bytes 524288 | tf_op jit(solution)/shard_map/all_to_all | solution.py:443
  40.9 0.9 %fold.1 = f32[4,32,64]{2,1,0:T(8,128)} custom-call(s16[32,2,16,128]{3,2,1,0:T(8,128)(2,1)S(1)} %all_to_all.5.codes, s32[1,32]{1,0:T(1,128)S(1)} %bitcast.5), custom_call_target="tpu_custom_call" | custom-call | tf_op jit(solution)/shard_map/fold/pallas_call | solution.py:396
Async XLA Ops:
  0.0 1.6 %copy-start = (bf16[16,32,2048]{2,1,0:T(8,128)(2,1)S(1)}, bf16[16,32,2048]{2,1,0:T(8,128)(2,1)}, u32[]{:S(2)}) copy-start(bf16[16,32,2048]{2,1,0:T(8,128)(2,1)} %vol.7) | copy-start | bytes 6291460
  1.6 3.3 %copy-start.1 = (s32[32]{0:T(128)S(1)}, s32[32]{0:T(128)}, u32[]{:S(2)}) copy-start(s32[32]{0:T(128)} %param.3) | copy-start | bytes 388
  2.3 4.9 %collective-permute-start = (bf16[17,16,2048]{2,1,0:T(8,128)(2,1)S(1)}, bf16[17,16,2048]{2,1,0:T(8,128)(2,1)S(1)}, u32[]{:S(2)}, u32[]{:S(2)}) collective-permute-start(bf16[17,16,2048]{2,1,0:T(8,128)(2,1)S(1)} %get-tuple-element.12), channel_id=1, source_target_pairs={{0,16},{16,0},{32,48},{48,32},{64,80},{80,64},{96,112},{112,96},{1... | collective-permute-start | bytes 3342344 | tf_op jit(solution)/shard_map/ppermute | solution.py:412
  7.5 12.0 %collective-permute-start.3 = (bf16[32,2048]{1,0:T(8,128)(2,1)S(1)}, bf16[32,2048]{1,0:T(8,128)(2,1)S(1)}, u32[]{:S(2)}, u32[]{:S(2)}) collective-permute-start(bf16[32,2048]{1,0:T(8,128)(2,1)S(1)} %get-tuple-element.15), channel_id=1, source_target_pairs={{16,1},{1,16},{17,2},{2,17},{18,3},{3,18},{19,4},{4,19},{20,5},{5,... | collective-permute-start | bytes 393224 | tf_op jit(solution)/shard_map/ppermute | solution.py:422
  12.6 10.4 %collective-permute-start.1 = (bf16[16,2048]{1,0:T(8,128)(2,1)S(1)}, bf16[16,2048]{1,0:T(8,128)(2,1)S(1)}, u32[]{:S(2)}, u32[]{:S(2)}) collective-permute-start(bf16[16,2048]{1,0:T(8,128)(2,1)S(1)} %get-tuple-element.13), channel_id=1, source_target_pairs={{0,32},{16,48},{32,64},{48,80},{64,96},{80,112},{96,128},{112,144}... | collective-permute-start | bytes 196616 | tf_op jit(solution)/shard_map/ppermute | solution.py:423
  15.8 7.2 %collective-permute-start.2 = (bf16[16,2048]{1,0:T(8,128)(2,1)S(1)}, bf16[16,2048]{1,0:T(8,128)(2,1)S(1)}, u32[]{:S(2)}, u32[]{:S(2)}) collective-permute-start(bf16[16,2048]{1,0:T(8,128)(2,1)S(1)} %get-tuple-element.14), channel_id=1, source_target_pairs={{32,0},{48,16},{64,32},{80,48},{96,64},{112,80},{128,96},{144,112}... | collective-permute-start | bytes 196616 | tf_op jit(solution)/shard_map/ppermute | solution.py:424

commit v5 on v4

--- a/solution.py
+++ b/solution.py
@@ -54,17 +54,16 @@
     return jnp.concatenate([ref[l, :, here].astype(F32)[row : row + 1] for l in range(16)], 0).astype(BF16)
 
 
-def share_kernel(vol, send, keep):
+def share_kernel(vol, send):
     layers, rows, depth = vol.shape
     half = rows // 2
 
-    def share(far, sent_row, kept_row):
+    def share(far, row):
         def tile(z, carry):
             here = lane_tile(LANES * z)
             for l in range(layers):
                 send[l, :, here] = vol[l, pl.ds(far, half), here]
-            send[layers, :, here] = one_row(vol, sent_row, here)
-            keep[:, here] = one_row(vol, kept_row, here)
+            send[layers, :, here] = one_row(vol, row, here)
             return carry
 
         lax.fori_loop(0, depth // LANES, tile, 0, unroll=2)
@@ -73,41 +72,62 @@
 
     @pl.when(core == 0)
     def _():
-        share(half, half - 1, half)
+        share(half, half - 1)
 
     @pl.when(core == 1)
     def _():
-        share(0, half, half - 1)
-
-
-def face_kernel(vol, mate, own, first, last, rim):
+        share(0, half)
+
+
+def own_faces(vol, core, end, rim):
     layers, rows, depth = vol.shape
     half = rows // 2
-    core = core_index()
-
-    @pl.when(core == 0)
-    def _():
+
+    def faces(layer, first, row):
         def tile(z, carry):
             here = lane_tile(LANES * z)
-            first[:, here] = vol[0, pl.ds(0, half), here]
+            end[:, here] = vol[layer, pl.ds(first, half), here]
+            rim[:, here] = one_row(vol, row, here)
+            return carry
+
+        lax.fori_loop(0, depth // LANES, tile, 0, unroll=2)
+
+    @pl.when(core == 0)
+    def _():
+        faces(0, 0, 0)
+
+    @pl.when(core == 1)
+    def _():
+        faces(layers - 1, half, rows - 1)
+
+
+def face_kernel(mate, own_end, own_rim, first, last, rim):
+    layers, half, depth = mate.shape[0] - 1, mate.shape[1], mate.shape[2]
+    core = core_index()
+
+    @pl.when(core == 0)
+    def _():
+        def tile(z, carry):
+            here = lane_tile(LANES * z)
+            first[:, here] = own_end[:, here]
             last[:, here] = mate[layers - 1, :, here]
-            rim[pl.ds(0, layers), here] = one_row(vol, 0, here)
+            rim[pl.ds(0, layers), here] = own_rim[:, here]
             rim[pl.ds(layers, layers), here] = one_row(mate, 0, here)
             return carry
 
-        lax.fori_loop(0, depth // LANES, tile, 0, unroll=2)
+        lax.fori_loop(0, depth // LANES, tile, 0, unroll=4)
 
     @pl.when(core == 1)
     def _():
         def tile(z, carry):
             here = lane_tile(LANES * z)
             first[:, here] = mate[0, :, here]
-            last[:, here] = vol[layers - 1, pl.ds(half, half), here]
+            last[:, here] = own_end[:, here]
             rim[pl.ds(0, layers), here] = one_row(mate, half - 1, here)
-            rim[pl.ds(layers, layers), here] = one_row(vol, rows - 1, here)
-            return carry
-
-        lax.fori_loop(0, depth // LANES, tile, 0, unroll=2)
+            rim[pl.ds(layers, layers), here] = own_rim[:, here]
+            return carry
+
+        lax.fori_loop(0, depth // LANES, tile, 0, unroll=4)
 
 
 class March:
@@ -183,69 +203,78 @@
     return rates.at[0, here], rates.at[1, here]
 
 
-def own_kernel(ray_length, vol, view, part, field, rates):
+def own_kernel(ray_length, vol, view, part, field, rates, end, rim):
     layers, rows, depth = vol.shape
-    tiles = depth // LANES
+    tiles, half = depth // LANES, rows // 2
     set_rates(view, ray_length, rates)
-
-    def widen(l, carry):
-        field[l, 0] = jnp.zeros((rows, LANES), F32)
-        field[l, tiles + 1] = jnp.zeros((rows, LANES), F32)
-        for tile in range(tiles):
-            field[l, tile + 1] = vol[l, :, pl.ds(LANES * tile, LANES)].astype(F32)
-        return carry
-
-    lax.fori_loop(0, layers, widen, 0)
-    row = pl.multiple_of(8 + 8 * core_index(), 8)
+    core = core_index()
+    own_faces(vol, core, end, rim)
+    mine = layers * core
+
+    def widen(first, beside):
+        def one(l, carry):
+            field[mine + l, 0] = jnp.zeros((rows, LANES), F32)
+            field[mine + l, tiles + 1] = jnp.zeros((rows, LANES), F32)
+            for tile in range(tiles):
+                here = pl.ds(LANES * tile, LANES)
+                field[mine + l, tile + 1, pl.ds(8, half), :] = vol[l, pl.ds(first, half), here].astype(F32)
+                near = vol[l, pl.ds(half - first, half), here].astype(F32)
+                field[mine + l, tile + 1, pl.ds(beside[1], 8), :] = near[beside[0] : beside[0] + 8]
+            return carry
+
+        lax.fori_loop(0, layers, one, 0)
+
+    @pl.when(core == 0)
+    def _():
+        widen(0, (0, half + 8))
+
+    @pl.when(core == 1)
+    def _():
+        widen(half, (half - 8, 0))
+
+    row = pl.multiple_of(16 - 8 * core, 8)
 
     def work(group, carry):
         march = March(field, group)
         state = march.fresh()
         for l in range(1, layers - 1):
-            march.layer(row, l, rates_of(rates, row), state)
+            march.layer(row, mine + l, rates_of(rates, 8 + 8 * core), state)
         march.keep(state, part)
         return carry
 
     lax.fori_loop(0, tiles // TILES, work, 0)
 
 
-def mate_kernel(ray_length, vol, mate, keep, view, part, field, rates):
-    layers, rows, depth = vol.shape
-    tiles, half = depth // LANES, rows // 2
-    set_rates(view, ray_length, rates)
+def mate_kernel(mate, rates, own_field, part, field):
+    layers, half, depth = mate.shape[0] - 1, mate.shape[1], mate.shape[2]
+    tiles = depth // LANES
     core = core_index()
     inside = pl.ds(8, half)
-    mine, other = layers * core, layers * (1 - core)
-    own_rows = pl.ds(pl.multiple_of(half * core, half), half)
+    other = layers * (1 - core)
 
     def widen(l, carry):
-        for index in (mine + l, other + l):
-            field[index, 0, inside, :] = jnp.zeros((half, LANES), F32)
-            field[index, tiles + 1, inside, :] = jnp.zeros((half, LANES), F32)
+        field[other + l, 0, inside, :] = jnp.zeros((half, LANES), F32)
+        field[other + l, tiles + 1, inside, :] = jnp.zeros((half, LANES), F32)
         for tile in range(tiles):
-            here = pl.ds(LANES * tile, LANES)
-            field[mine + l, tile + 1, inside, :] = vol[l, own_rows, here].astype(F32)
-            field[other + l, tile + 1, inside, :] = mate[l, :, here].astype(F32)
+            field[other + l, tile + 1, inside, :] = mate[l, :, pl.ds(LANES * tile, LANES)].astype(F32)
         return carry
 
     lax.fori_loop(0, layers, widen, 0)
 
-    def border(slot, mine, other):
+    def border(slot, other):
         def tile(z, carry):
-            here = lane_tile(LANES * z)
-            field[pl.ds(mine, layers), z + 1, slot, :] = keep[:, here].astype(F32)
-            field[pl.ds(other, layers), z + 1, slot, :] = mate[layers, :, here].astype(F32)
+            field[pl.ds(other, layers), z + 1, slot, :] = mate[layers, :, lane_tile(LANES * z)].astype(F32)
             return carry
 
         lax.fori_loop(0, tiles, tile, 0, unroll=2)
 
     @pl.when(core == 0)
     def _():
-        border(half + 8, 0, layers)
+        border(half + 8, layers)
 
     @pl.when(core == 1)
     def _():
-        border(7, layers, 0)
+        border(7, 0)
 
     row = pl.multiple_of(16 - 8 * core, 8)
     begin = layers - 1 - (layers - 2) * core
@@ -266,10 +295,9 @@
     return rows_down == 8 * core, rows_down == 8 - core
 
 
-def rim_kernel(ray_length, beyond, view, field, part, rates, beyond_wide):
+def rim_kernel(beyond, rates, field, part, beyond_wide):
     layers = field.shape[0]
     tiles = part.shape[2] // LANES
-    set_rates(view, ray_length, rates)
     beyond_wide[...] = beyond[...].astype(F32)
     core = core_index()
     above, below = rim_masks(core)
@@ -286,10 +314,9 @@
     lax.fori_loop(0, tiles // TILES, work, 0)
 
 
-def outer_kernel(ray_length, before, after, beyond, view, own, other, border, field, codes, rates, before_wide, after_wide, beyond_wide, levels):
+def outer_kernel(before, after, beyond, rates, own, other, border, field, codes, before_wide, after_wide, beyond_wide, levels):
     layers = field.shape[0]
     tiles = own.shape[2] // LANES
-    set_rates(view, ray_length, rates)
     before_wide[...] = before[...].astype(F32)
     after_wide[...] = after[...].astype(F32)
     beyond_wide[...] = beyond[...].astype(F32)
@@ -392,51 +419,44 @@
     in_vmem = pl.BlockSpec(memory_space=pltpu.VMEM)
     shape = jax.ShapeDtypeStruct
 
-    def call(kernel, operands, out_shape, scratch, name, cost=0, limit=24):
+    def call(kernel, operands, out_shape, scratch, name, cost=0, limit=24, aliases={}):
         return pl.pallas_call(
             kernel,
             out_shape=out_shape,
             in_specs=[in_vmem] * len(operands),
             out_specs=jax.tree.map(lambda _: in_vmem, out_shape),
             scratch_shapes=scratch,
+            input_output_aliases=aliases,
             compiler_params=pltpu.CompilerParams(vmem_limit_bytes=limit << 20),
             cost_estimate=pl.CostEstimate(flops=cost, bytes_accessed=2 * layers * rows * depth, transcendentals=0) if cost else None,
             name=name,
         )(*operands)
 
     work = 40 * layers * half * depth
-    length = layers * size_x
-    rates = pltpu.VMEM((2, rows, LANES), F32)
     face, part = shape((half, depth), BF16), shape((5, 8, depth), F32)
-    send, keep = call(share_kernel, (volume,), (shape((layers + 1, half, depth), BF16), face), [], "share")
+    brick = shape((2 * layers, depth // LANES + 2, half + 16, LANES), F32)
+    send = call(share_kernel, (volume,), shape((layers + 1, half, depth), BF16), [], "share")
     mate = lax.ppermute(send, "bx", mates)
-    own = call(
-        functools.partial(own_kernel, length),
+    own, field, rates, own_end, own_rim = call(
+        functools.partial(own_kernel, layers * size_x),
         (volume, view),
-        part,
-        [pltpu.VMEM((layers, depth // LANES + 2, rows, LANES), F32), rates],
+        (part, brick, shape((2, rows, LANES), F32), face, face),
+        [],
         "own",
         work // 2,
     )
-    first, last, rim = call(face_kernel, (volume, mate, own), (face, face, shape((2 * layers, depth), BF16)), [], "face")
+    first, last, rim = call(face_kernel, (mate, own_end, own_rim), (face, face, shape((2 * layers, depth), BF16)), [], "face")
     beyond = lax.ppermute(rim, ("bx", "by"), across)
     before = lax.ppermute(last, "bx", up_x)
     after = lax.ppermute(first, "bx", down_x)
-    other, field = call(
-        functools.partial(mate_kernel, length),
-        (volume, mate, keep, view),
-        (part, shape((2 * layers, depth // LANES + 2, half + 16, LANES), F32)),
-        [rates],
-        "mate",
-        work // 2,
-    )
+    other, field = call(mate_kernel, (mate, rates, field), (part, brick), [], "mate", work // 2, aliases={2: 1})
     wide, rim_wide = pltpu.VMEM((half, depth), F32), pltpu.VMEM((2 * layers, depth), F32)
-    border = call(functools.partial(rim_kernel, length), (beyond, view, field), part, [rates, rim_wide], "rim", work)
+    border = call(rim_kernel, (beyond, rates, field), part, [rim_wide], "rim", work)
     codes = call(
-        functools.partial(outer_kernel, length),
-        (before, after, beyond, view, own, other, border, field),
+        outer_kernel,
+        (before, after, beyond, rates, own, other, border, field),
         shape((size_x, 2, 16, LANES), jnp.int16),
-        [rates, wide, wide, rim_wide, pltpu.VMEM((4, TILES, 16, LANES), jnp.int32)],
+        [wide, wide, rim_wide, pltpu.VMEM((4, TILES, 16, LANES), jnp.int32)],
         "outer",
         work,
     )

time: 42.1 us -> 41.2 us (0.979)
  Pallas kernels: 10.9 us -> 10.1 us
    pallas_call x7, Pallas kernels: 10.9 us -> 10.1 us  [call(): pl.pallas_call(kernel, out_shape=out_shape, in_specs=[in_vmem] * len(oper...]
  transfers between devices with their start and end apart: 4 -> 4, of which waited for: 1 -> 1; matrix products, arithmetic and copies ran while one was open for 0% -> 0% of each run, Pallas kernels for 19% -> 18%
where the time goes in v5:
time: 41.2 us; the launch traced here: 41 us
  blocking collectives  16.8 us (41%)
  starting transfers between devices  12.1 us (29%)
  Pallas kernels  10.1 us (25%)
  local copies, waits for them, and re-layouts  1.59 us (4%)
    all_to_all x1, blocking collectives, body(): codes = lax.all_to_all(codes, 'bx', split_axis=0, concat_axis=0, tiled=True)  16.8 us
    pallas_call x7, Pallas kernels, call(): pl.pallas_call(kernel, out_shape=out_shape, in_specs=[in_vmem] * len(oper...  10.1 us
    ppermute x1, starting transfers between devices, body(): beyond = lax.ppermute(rim, ('bx', 'by'), across)  5.02 us
    ppermute x1, starting transfers between devices, body(): before = lax.ppermute(last, 'bx', up_x)  3.2 us
    ppermute x1, starting transfers between devices, body(): mate = lax.ppermute(send, 'bx', mates)  2.58 us
    unnamed x4, local copies, waits for them, and re-layouts  1.59 us
    ppermute x1, starting transfers between devices, body(): after = lax.ppermute(first, 'bx', down_x)  1.29 us
  transfers between devices with their start and end apart: 4, of which 1 were waited for; matrix products, arithmetic and copies ran while one was open for 0% of the time, Pallas kernels for 18%

profile of v5, /device:TPU:225, one launch (start us, length us, event | category | flops | bytes accessed | tf_op | source)
XLA Modules:
  0.0 41.0 jit_solution(16568602651038774424)
XLA Ops:
  0.0 0.0 copy-start
  0.0 1.6 %copy-done = bf16[16,32,2048]{2,1,0:T(8,128)(2,1)S(1)} copy-done((bf16[16,32,2048]{2,1,0:T(8,128)(2,1)S(1)}, bf16[16,32,2048]{2,1,0:T(8,128)(2,1)}, u32[]{:S(2)}) %copy-start) | copy-done | bytes 2097176
  1.6 0.0 copy-start.1
  1.6 0.4 %share.1 = bf16[17,16,2048]{2,1,0:T(8,128)(2,1)S(1)} custom-call(bf16[16,32,2048]{2,1,0:T(8,128)(2,1)S(1)} %copy-done), custom_call_target="tpu_custom_call" | custom-call | tf_op jit(solution)/shard_map/share/pallas_call | solution.py:423
  2.0 2.6 %collective-permute-start = (bf16[17,16,2048]{2,1,0:T(8,128)(2,1)S(1)}, bf16[17,16,2048]{2,1,0:T(8,128)(2,1)S(1)}, u32[]{:S(2)}, u32[]{:S(2)}) collective-permute-start(bf16[17,16,2048]{2,1,0:T(8,128)(2,1)S(1)} %share.1), channel_id=1, source_target_pairs={{0,16},{16,0},{32,48},{48,32},{64,80},{80,64},{96,112},{112,96},{1... | collective-permute-start | bytes 3342344 | tf_op jit(solution)/shard_map/ppermute | solution.py:439
  4.6 0.0 copy-done.1
  4.6 2.0 %own.1 = (f32[5,8,2048]{2,1,0:T(8,128)S(1)}, f32[32,18,32,128]{3,2,1,0:T(8,128)S(1)}, f32[2,32,128]{2,1,0:T(8,128)S(1)}, bf16[16,2048]{1,0:T(8,128)(2,1)S(1)}, bf16[16,2048]{1,0:T(8,128)(2,1)S(1)}) custom-call(bf16[16,32,2048]{2,1,0:T(8,128)(2,1)S(1)} %copy-done, s32[1,32]{1,0:T(1,128)S(1)} %bitcast.1), custom_call_target="tpu_custom_call" | custom-call | flops 10485760 | bytes 2097152 | tf_op jit(solution)/shard_map/own/pallas_call | solution.py:423
  6.7 0.3 collective-permute-done.mate
  7.0 0.2 face.1
  7.2 5.0 %collective-permute-start.3 = (bf16[32,2048]{1,0:T(8,128)(2,1)S(1)}, bf16[32,2048]{1,0:T(8,128)(2,1)S(1)}, u32[]{:S(2)}, u32[]{:S(2)}) collective-permute-start(bf16[32,2048]{1,0:T(8,128)(2,1)S(1)} %get-tuple-element.19), channel_id=1, source_target_pairs={{16,1},{1,16},{17,2},{2,17},{18,3},{3,18},{19,4},{4,19},{20,5},{5,... | collective-permute-start | bytes 393224 | tf_op jit(solution)/shard_map/ppermute | solution.py:449
  12.2 3.2 %collective-permute-start.1 = (bf16[16,2048]{1,0:T(8,128)(2,1)S(1)}, bf16[16,2048]{1,0:T(8,128)(2,1)S(1)}, u32[]{:S(2)}, u32[]{:S(2)}) collective-permute-start(bf16[16,2048]{1,0:T(8,128)(2,1)S(1)} %get-tuple-element.17), channel_id=1, source_target_pairs={{0,32},{16,48},{32,64},{48,80},{64,96},{80,112},{96,128},{112,144}... | collective-permute-start | bytes 196616 | tf_op jit(solution)/shard_map/ppermute | solution.py:450
  15.4 1.3 %collective-permute-start.2 = (bf16[16,2048]{1,0:T(8,128)(2,1)S(1)}, bf16[16,2048]{1,0:T(8,128)(2,1)S(1)}, u32[]{:S(2)}, u32[]{:S(2)}) collective-permute-start(bf16[16,2048]{1,0:T(8,128)(2,1)S(1)} %get-tuple-element.18), channel_id=1, source_target_pairs={{32,0},{48,16},{64,32},{80,48},{96,64},{112,80},{128,96},{144,112}... | collective-permute-start | bytes 196616 | tf_op jit(solution)/shard_map/ppermute | solution.py:451
  16.7 2.1 %mate.1 = (f32[5,8,2048]{2,1,0:T(8,128)S(1)}, f32[32,18,32,128]{3,2,1,0:T(8,128)S(1)}) custom-call(bf16[17,16,2048]{2,1,0:T(8,128)(2,1)S(1)} %collective-permute-done.mate, f32[2,32,128]{2,1,0:T(8,128)S(1)} %get-tuple-element.20.rates, f32[32,18,32,128]{3,2,1,0:T(8,128)S(1)} %get-tuple-element.22.own_field), custom_call_target="tpu_custom_call", output_to_operand_aliasing={{1}: (2, {})} | custom-call | flops 10485760 | bytes 2097152 | tf_op jit(solution)/shard_map/mate/pallas_call | solution.py:423
  18.8 0.0 collective-permute-done.3.beyond
  18.8 3.4 %rim.1.border = f32[5,8,2048]{2,1,0:T(8,128)S(1)} custom-call(bf16[32,2048]{1,0:T(8,128)(2,1)S(1)} %collective-permute-done.3.beyond, f32[2,32,128]{2,1,0:T(8,128)S(1)} %get-tuple-element.20.rates, f32[32,18,32,128]{3,2,1,0:T(8,128)S(1)} %get-tuple-element.24.field), custom_call_target="tpu_custom_call" | custom-call | flops 20971520 | bytes 2097152 | tf_op jit(solution)/shard_map/rim/pallas_call | solution.py:423
  22.2 0.0 collective-permute-done.1.before
  22.2 0.0 collective-permute-done.2.after
  22.2 1.1 %outer.1 = s16[32,2,16,128]{3,2,1,0:T(8,128)(2,1)S(1)} custom-call(bf16[16,2048]{1,0:T(8,128)(2,1)S(1)} %collective-permute-done.1.before, bf16[16,2048]{1,0:T(8,128)(2,1)S(1)} %collective-permute-done.2.after, bf16[32,2048]{1,0:T(8,128)(2,1)S(1)} %collective-permute-done.3.beyond, f32[2,32,128]{2,1,0:T(8,128)S(1)} %get-tuple-element.20.rates, ...), custom_call_target="tpu_custom_call" | custom-call | flops 20971520 | bytes 2097152 | tf_op jit(solution)/shard_map/outer/pallas_call | solution.py:423
  23.3 16.8 %all_to_all.5.codes = s16[32,2,16,128]{3,2,1,0:T(8,128)(2,1)S(1)} all-to-all(s16[32,2,16,128]{3,2,1,0:T(8,128)(2,1)S(1)} %outer.1), channel_id=1, replica_groups=mesh['bx'=32,'by'=16] {'bx'}, dimensions={0} | all-to-all | bytes 524288 | tf_op jit(solution)/shard_map/all_to_all | solution.py:463
  40.1 0.9 %fold.1 = f32[4,32,64]{2,1,0:T(8,128)} custom-call(s16[32,2,16,128]{3,2,1,0:T(8,128)(2,1)S(1)} %all_to_all.5.codes, s32[1,32]{1,0:T(1,128)S(1)} %bitcast.2), custom_call_target="tpu_custom_call" | custom-call | tf_op jit(solution)/shard_map/fold/pallas_call | solution.py:423
Async XLA Ops:
  0.0 1.6 %copy-start = (bf16[16,32,2048]{2,1,0:T(8,128)(2,1)S(1)}, bf16[16,32,2048]{2,1,0:T(8,128)(2,1)}, u32[]{:S(2)}) copy-start(bf16[16,32,2048]{2,1,0:T(8,128)(2,1)} %vol.3) | copy-start | bytes 6291460
  1.6 3.0 %copy-start.1 = (s32[32]{0:T(128)S(1)}, s32[32]{0:T(128)}, u32[]{:S(2)}) copy-start(s32[32]{0:T(128)} %param.3) | copy-start | bytes 388
  2.0 4.9 %collective-permute-start = (bf16[17,16,2048]{2,1,0:T(8,128)(2,1)S(1)}, bf16[17,16,2048]{2,1,0:T(8,128)(2,1)S(1)}, u32[]{:S(2)}, u32[]{:S(2)}) collective-permute-start(bf16[17,16,2048]{2,1,0:T(8,128)(2,1)S(1)} %share.1), channel_id=1, source_target_pairs={{0,16},{16,0},{32,48},{48,32},{64,80},{80,64},{96,112},{112,96},{1... | collective-permute-start | bytes 3342344 | tf_op jit(solution)/shard_map/ppermute | solution.py:439
  7.2 11.6 %collective-permute-start.3 = (bf16[32,2048]{1,0:T(8,128)(2,1)S(1)}, bf16[32,2048]{1,0:T(8,128)(2,1)S(1)}, u32[]{:S(2)}, u32[]{:S(2)}) collective-permute-start(bf16[32,2048]{1,0:T(8,128)(2,1)S(1)} %get-tuple-element.19), channel_id=1, source_target_pairs={{16,1},{1,16},{17,2},{2,17},{18,3},{3,18},{19,4},{4,19},{20,5},{5,... | collective-permute-start | bytes 393224 | tf_op jit(solution)/shard_map/ppermute | solution.py:449
  12.2 10.0 %collective-permute-start.1 = (bf16[16,2048]{1,0:T(8,128)(2,1)S(1)}, bf16[16,2048]{1,0:T(8,128)(2,1)S(1)}, u32[]{:S(2)}, u32[]{:S(2)}) collective-permute-start(bf16[16,2048]{1,0:T(8,128)(2,1)S(1)} %get-tuple-element.17), channel_id=1, source_target_pairs={{0,32},{16,48},{32,64},{48,80},{64,96},{80,112},{96,128},{112,144}... | collective-permute-start | bytes 196616 | tf_op jit(solution)/shard_map/ppermute | solution.py:450
  15.4 6.8 %collective-permute-start.2 = (bf16[16,2048]{1,0:T(8,128)(2,1)S(1)}, bf16[16,2048]{1,0:T(8,128)(2,1)S(1)}, u32[]{:S(2)}, u32[]{:S(2)}) collective-permute-start(bf16[16,2048]{1,0:T(8,128)(2,1)S(1)} %get-tuple-element.18), channel_id=1, source_target_pairs={{32,0},{48,16},{64,32},{80,48},{96,64},{112,80},{128,96},{144,112}... | collective-permute-start | bytes 196616 | tf_op jit(solution)/shard_map/ppermute | solution.py:451

commit v6 on v5

--- a/solution.py
+++ b/solution.py
@@ -54,7 +54,19 @@
     return jnp.concatenate([ref[l, :, here].astype(F32)[row : row + 1] for l in range(16)], 0).astype(BF16)
 
 
-def share_kernel(vol, send):
+def end_kernel(vol, end):
+    depth = vol.shape[2]
+    layer = (vol.shape[0] - 1) * core_index()
+
+    def tile(z, carry):
+        here = lane_tile(LANES * z)
+        end[:, here] = vol[layer, :, here]
+        return carry
+
+    lax.fori_loop(0, depth // LANES, tile, 0, unroll=8)
+
+
+def share_kernel(vol, end, send):
     layers, rows, depth = vol.shape
     half = rows // 2
 
@@ -79,14 +91,12 @@
         share(0, half)
 
 
-def own_faces(vol, core, end, rim):
-    layers, rows, depth = vol.shape
-    half = rows // 2
-
-    def faces(layer, first, row):
+def own_edge(vol, core, rim):
+    rows, depth = vol.shape[1], vol.shape[2]
+
+    def edge(row):
         def tile(z, carry):
             here = lane_tile(LANES * z)
-            end[:, here] = vol[layer, pl.ds(first, half), here]
             rim[:, here] = one_row(vol, row, here)
             return carry
 
@@ -94,40 +104,46 @@
 
     @pl.when(core == 0)
     def _():
-        faces(0, 0, 0)
-
-    @pl.when(core == 1)
-    def _():
-        faces(layers - 1, half, rows - 1)
-
-
-def face_kernel(mate, own_end, own_rim, first, last, rim):
+        edge(0)
+
+    @pl.when(core == 1)
+    def _():
+        edge(rows - 1)
+
+
+def rim_rows_kernel(mate, own_rim, rim):
     layers, half, depth = mate.shape[0] - 1, mate.shape[1], mate.shape[2]
-    core = core_index()
-
-    @pl.when(core == 0)
-    def _():
+
+    def edge(own_at, mate_at, row):
         def tile(z, carry):
             here = lane_tile(LANES * z)
-            first[:, here] = own_end[:, here]
-            last[:, here] = mate[layers - 1, :, here]
-            rim[pl.ds(0, layers), here] = own_rim[:, here]
-            rim[pl.ds(layers, layers), here] = one_row(mate, 0, here)
+            rim[pl.ds(own_at, layers), here] = own_rim[:, here]
+            rim[pl.ds(mate_at, layers), here] = one_row(mate, row, here)
             return carry
 
         lax.fori_loop(0, depth // LANES, tile, 0, unroll=4)
 
-    @pl.when(core == 1)
-    def _():
-        def tile(z, carry):
-            here = lane_tile(LANES * z)
-            first[:, here] = mate[0, :, here]
-            last[:, here] = own_end[:, here]
-            rim[pl.ds(0, layers), here] = one_row(mate, half - 1, here)
-            rim[pl.ds(layers, layers), here] = own_rim[:, here]
-            return carry
-
-        lax.fori_loop(0, depth // LANES, tile, 0, unroll=4)
+    core = core_index()
+
+    @pl.when(core == 0)
+    def _():
+        edge(0, layers, 0)
+
+    @pl.when(core == 1)
+    def _():
+        edge(layers, 0, half - 1)
+
+
+def hand_kernel(face, rim, hand_on):
+    half, depth = hand_on.shape
+    far = pl.multiple_of(half - half * core_index(), half)
+
+    def tile(z, carry):
+        here = lane_tile(LANES * z)
+        hand_on[:, here] = face[pl.ds(far, half), here]
+        return carry
+
+    lax.fori_loop(0, depth // LANES, tile, 0, unroll=8)
 
 
 class March:
@@ -203,12 +219,12 @@
     return rates.at[0, here], rates.at[1, here]
 
 
-def own_kernel(ray_length, vol, view, part, field, rates, end, rim):
+def own_kernel(ray_length, vol, view, part, field, rates, rim):
     layers, rows, depth = vol.shape
     tiles, half = depth // LANES, rows // 2
     set_rates(view, ray_length, rates)
     core = core_index()
-    own_faces(vol, core, end, rim)
+    own_edge(vol, core, rim)
     mine = layers * core
 
     def widen(first, beside):
@@ -314,13 +330,23 @@
     lax.fori_loop(0, tiles // TILES, work, 0)
 
 
-def outer_kernel(before, after, beyond, rates, own, other, border, field, codes, before_wide, after_wide, beyond_wide, levels):
+def outer_kernel(face, handed, beyond, rates, own, other, border, field, codes, before_wide, after_wide, beyond_wide, levels):
     layers = field.shape[0]
     tiles = own.shape[2] // LANES
-    before_wide[...] = before[...].astype(F32)
-    after_wide[...] = after[...].astype(F32)
     beyond_wide[...] = beyond[...].astype(F32)
     core = core_index()
+    half = before_wide.shape[0]
+
+    @pl.when(core == 0)
+    def _():
+        before_wide[...] = face[pl.ds(0, half)].astype(F32)
+        after_wide[...] = handed[...].astype(F32)
+
+    @pl.when(core == 1)
+    def _():
+        before_wide[...] = handed[...].astype(F32)
+        after_wide[...] = face[pl.ds(half, half)].astype(F32)
+
     above, below = rim_masks(core)
     own_first = jnp.zeros((8, LANES), jnp.int32) + core == 0
     low = lax.broadcasted_iota(jnp.int32, (8, LANES), 1) < LANES // 2
@@ -408,8 +434,8 @@
     size_x, size_y = lax.axis_size("bx"), lax.axis_size("by")
     half = rows // 2
     mates = [(i, i ^ 1) for i in range(size_x)]
-    up_x = [(i, i + 2) for i in range(size_x - 2)]
-    down_x = [(j, i) for i, j in up_x]
+    chips = [(i, i + 1) for i in range(1, size_x - 1, 2)]
+    chips += [(j, i) for i, j in chips]
     across = []
     for i in range(0, size_x, 2):
         for j in range(size_y - 1):
@@ -435,26 +461,28 @@
     work = 40 * layers * half * depth
     face, part = shape((half, depth), BF16), shape((5, 8, depth), F32)
     brick = shape((2 * layers, depth // LANES + 2, half + 16, LANES), F32)
-    send = call(share_kernel, (volume,), shape((layers + 1, half, depth), BF16), [], "share")
+    end = call(end_kernel, (volume,), shape((rows, depth), BF16), [], "end")
+    end_in = lax.ppermute(end, "bx", chips)
+    send = call(share_kernel, (volume, end), shape((layers + 1, half, depth), BF16), [], "share")
     mate = lax.ppermute(send, "bx", mates)
-    own, field, rates, own_end, own_rim = call(
+    own, field, rates, own_rim = call(
         functools.partial(own_kernel, layers * size_x),
         (volume, view),
-        (part, brick, shape((2, rows, LANES), F32), face, face),
+        (part, brick, shape((2, rows, LANES), F32), face),
         [],
         "own",
         work // 2,
     )
-    first, last, rim = call(face_kernel, (mate, own_end, own_rim), (face, face, shape((2 * layers, depth), BF16)), [], "face")
+    rim = call(rim_rows_kernel, (mate, own_rim), shape((2 * layers, depth), BF16), [], "rim_rows")
     beyond = lax.ppermute(rim, ("bx", "by"), across)
-    before = lax.ppermute(last, "bx", up_x)
-    after = lax.ppermute(first, "bx", down_x)
+    hand_on = call(hand_kernel, (end_in, rim), face, [], "hand")
+    handed = lax.ppermute(hand_on, "bx", mates)
     other, field = call(mate_kernel, (mate, rates, field), (part, brick), [], "mate", work // 2, aliases={2: 1})
     wide, rim_wide = pltpu.VMEM((half, depth), F32), pltpu.VMEM((2 * layers, depth), F32)
     border = call(rim_kernel, (beyond, rates, field), part, [rim_wide], "rim", work)
     codes = call(
         outer_kernel,
-        (before, after, beyond, rates, own, other, border, field),
+        (end_in, handed, beyond, rates, own, other, border, field),
         shape((size_x, 2, 16, LANES), jnp.int16),
         [wide, wide, rim_wide, pltpu.VMEM((4, TILES, 16, LANES), jnp.int32)],
         "outer",

time: 41.2 us -> 40.2 us (0.976)
  starting transfers between devices: 12.1 us -> 9.8 us
  waiting for transfers between devices: 0.31 us -> 1.21 us
    ppermute x1, starting transfers between devices: 5.02 us -> 2.2 us  [body(): beyond = lax.ppermute(rim, ('bx', 'by'), across)]
    ppermute x1, waiting for transfers between devices: 0.01 us -> 1.2 us  [body(): beyond = lax.ppermute(rim, ('bx', 'by'), across)]
    ppermute x2, starting transfers between devices: 4.5 us -> 5.02 us  [the longest x1 3.1 us: body(): end_in = lax.ppermute(end, 'bx', chips)]
    pallas_call x7 -> x9, Pallas kernels: 10.1 us -> 10.2 us  [call(): pl.pallas_call(kernel, out_shape=out_shape, in_specs=[in_vmem] * len(oper...]
  transfers between devices with their start and end apart: 4 -> 4, of which waited for: 1 -> 1; matrix products, arithmetic and copies ran while one was open for 0% -> 0% of each run, Pallas kernels for 18% -> 19%
where the time goes in v6:
time: 40.2 us; the launch traced here: 40 us
  blocking collectives  17 us (42%)
  Pallas kernels  10.2 us (25%)
  starting transfers between devices  9.8 us (24%)
  local copies, waits for them, and re-layouts  1.6 us (4%)
  waiting for transfers between devices  1.21 us (3%)
    all_to_all x1, blocking collectives, body(): codes = lax.all_to_all(codes, 'bx', split_axis=0, concat_axis=0, tiled=True)  17 us
    pallas_call x9, Pallas kernels, call(): pl.pallas_call(kernel, out_shape=out_shape, in_specs=[in_vmem] * len(oper...  10.2 us
    ppermute x1, starting transfers between devices, body(): end_in = lax.ppermute(end, 'bx', chips)  3.1 us
    ppermute x1, starting transfers between devices, body(): mate = lax.ppermute(send, 'bx', mates)  2.57 us
    ppermute x1, starting transfers between devices, body(): beyond = lax.ppermute(rim, ('bx', 'by'), across)  2.2 us
    ppermute x1, starting transfers between devices, body(): handed = lax.ppermute(hand_on, 'bx', mates)  1.92 us
    unnamed x4, local copies, waits for them, and re-layouts  1.6 us
    ppermute x1, waiting for transfers between devices, body(): beyond = lax.ppermute(rim, ('bx', 'by'), across)  1.2 us
  transfers between devices with their start and end apart: 4, of which 1 were waited for; matrix products, arithmetic and copies ran while one was open for 0% of the time, Pallas kernels for 19%

profile of v6, /device:TPU:225, one launch (start us, length us, event | category | flops | bytes accessed | tf_op | source)
XLA Modules:
  0.0 40.0 jit_solution(8605142240590178713)
XLA Ops:
  0.0 0.0 copy-start
  0.0 1.6 %copy-done = bf16[16,32,2048]{2,1,0:T(8,128)(2,1)S(1)} copy-done((bf16[16,32,2048]{2,1,0:T(8,128)(2,1)S(1)}, bf16[16,32,2048]{2,1,0:T(8,128)(2,1)}, u32[]{:S(2)}) %copy-start) | copy-done | bytes 2097176
  1.6 0.0 copy-start.1
  1.7 0.5 %share.1 = bf16[17,16,2048]{2,1,0:T(8,128)(2,1)S(1)} custom-call(bf16[16,32,2048]{2,1,0:T(8,128)(2,1)S(1)} %copy-done, bf16[32,2048]{1,0:T(8,128)(2,1)S(1)} %end.1), custom_call_target="tpu_custom_call" | custom-call | tf_op jit(solution)/shard_map/share/pallas_call | solution.py:449
  2.1 2.6 %collective-permute-start.1 = (bf16[17,16,2048]{2,1,0:T(8,128)(2,1)S(1)}, bf16[17,16,2048]{2,1,0:T(8,128)(2,1)S(1)}, u32[]{:S(2)}, u32[]{:S(2)}) collective-permute-start(bf16[17,16,2048]{2,1,0:T(8,128)(2,1)S(1)} %share.1), channel_id=1, source_target_pairs={{0,16},{16,0},{32,48},{48,32},{64,80},{80,64},{96,112},{112,96},{1... | collective-permute-start | bytes 3342344 | tf_op jit(solution)/shard_map/ppermute | solution.py:467
  4.7 3.1 %collective-permute-start = (bf16[32,2048]{1,0:T(8,128)(2,1)S(1)}, bf16[32,2048]{1,0:T(8,128)(2,1)S(1)}, u32[]{:S(2)}, u32[]{:S(2)}) collective-permute-start(bf16[32,2048]{1,0:T(8,128)(2,1)S(1)} %end.1), channel_id=1, source_target_pairs={{16,32},{48,64},{80,96},{112,128},{144,160},{176,192},{208,224},{2... | collective-permute-start | bytes 393224 | tf_op jit(solution)/shard_map/ppermute | solution.py:465
  7.8 0.0 copy-done.1
  7.8 2.0 %own.1 = (f32[5,8,2048]{2,1,0:T(8,128)S(1)}, f32[32,18,32,128]{3,2,1,0:T(8,128)S(1)}, f32[2,32,128]{2,1,0:T(8,128)S(1)}, bf16[16,2048]{1,0:T(8,128)(2,1)S(1)}) custom-call(bf16[16,32,2048]{2,1,0:T(8,128)(2,1)S(1)} %copy-done, s32[1,32]{1,0:T(1,128)S(1)} %bitcast.1), custom_call_target="tpu_custom_call" | custom-call | flops 10485760 | bytes 2097152 | tf_op jit(solution)/shard_map/own/pallas_call | solution.py:449
  9.9 0.0 collective-permute-done.1.mate
  9.9 0.2 rim_rows.1.rim
  10.1 2.2 %collective-permute-start.3 = (bf16[32,2048]{1,0:T(8,128)(2,1)S(1)}, bf16[32,2048]{1,0:T(8,128)(2,1)S(1)}, u32[]{:S(2)}, u32[]{:S(2)}) collective-permute-start(bf16[32,2048]{1,0:T(8,128)(2,1)S(1)} %rim_rows.1.rim), channel_id=1, source_target_pairs={{16,1},{1,16},{17,2},{2,17},{18,3},{3,18},{19,4},{4,19},{20,5},{5,... | collective-permute-start | bytes 393224 | tf_op jit(solution)/shard_map/ppermute | solution.py:477
  12.3 0.0 collective-permute-done.face
  12.3 0.1 hand.1
  12.4 1.9 %collective-permute-start.2 = (bf16[16,2048]{1,0:T(8,128)(2,1)S(1)}, bf16[16,2048]{1,0:T(8,128)(2,1)S(1)}, u32[]{:S(2)}, u32[]{:S(2)}) collective-permute-start(bf16[16,2048]{1,0:T(8,128)(2,1)S(1)} %hand.1), channel_id=1, source_target_pairs={{0,16},{16,0},{32,48},{48,32},{64,80},{80,64},{96,112},{112,96},{1... | collective-permute-start | bytes 196616 | tf_op jit(solution)/shard_map/ppermute | solution.py:479
  14.3 2.1 %mate.1 = (f32[5,8,2048]{2,1,0:T(8,128)S(1)}, f32[32,18,32,128]{3,2,1,0:T(8,128)S(1)}) custom-call(bf16[17,16,2048]{2,1,0:T(8,128)(2,1)S(1)} %collective-permute-done.1.mate, f32[2,32,128]{2,1,0:T(8,128)S(1)} %get-tuple-element.12.rates, f32[32,18,32,128]{3,2,1,0:T(8,128)S(1)} %get-tuple-element.14.own_field), custom_call_target="tpu_custom_call", output_to_operand_aliasing={{1}: (2, {})} | custom-call | flops 10485760 | bytes 2097152 | tf_op jit(solution)/shard_map/mate/pallas_call | solution.py:449
  16.4 1.2 %collective-permute-done.3.beyond = bf16[32,2048]{1,0:T(8,128)(2,1)S(1)} collective-permute-done((bf16[32,2048]{1,0:T(8,128)(2,1)S(1)}, bf16[32,2048]{1,0:T(8,128)(2,1)S(1)}, u32[]{:S(2)}, u32[]{:S(2)}) %collective-permute-start.3) | collective-permute-done | bytes 131104 | tf_op jit(solution)/shard_map/ppermute | solution.py:477
  17.6 3.4 %rim.1.border = f32[5,8,2048]{2,1,0:T(8,128)S(1)} custom-call(bf16[32,2048]{1,0:T(8,128)(2,1)S(1)} %collective-permute-done.3.beyond, f32[2,32,128]{2,1,0:T(8,128)S(1)} %get-tuple-element.12.rates, f32[32,18,32,128]{3,2,1,0:T(8,128)S(1)} %get-tuple-element.16.field), custom_call_target="tpu_custom_call" | custom-call | flops 20971520 | bytes 2097152 | tf_op jit(solution)/shard_map/rim/pallas_call | solution.py:449
  21.0 0.0 collective-permute-done.2.handed
  21.0 1.1 %outer.1 = s16[32,2,16,128]{3,2,1,0:T(8,128)(2,1)S(1)} custom-call(bf16[32,2048]{1,0:T(8,128)(2,1)S(1)} %collective-permute-done.face, bf16[16,2048]{1,0:T(8,128)(2,1)S(1)} %collective-permute-done.2.handed, bf16[32,2048]{1,0:T(8,128)(2,1)S(1)} %collective-permute-done.3.beyond, f32[2,32,128]{2,1,0:T(8,128)S(1)} %get-tuple-element.12.rates, ...), custom_call_target="tpu_custom_call" | custom-call | flops 20971520 | bytes 2097152 | tf_op jit(solution)/shard_map/outer/pallas_call | solution.py:449
  22.1 17.0 %all_to_all.5.codes = s16[32,2,16,128]{3,2,1,0:T(8,128)(2,1)S(1)} all-to-all(s16[32,2,16,128]{3,2,1,0:T(8,128)(2,1)S(1)} %outer.1), channel_id=1, replica_groups=mesh['bx'=32,'by'=16] {'bx'}, dimensions={0} | all-to-all | bytes 524288 | tf_op jit(solution)/shard_map/all_to_all | solution.py:491
  39.1 0.9 %fold.1 = f32[4,32,64]{2,1,0:T(8,128)} custom-call(s16[32,2,16,128]{3,2,1,0:T(8,128)(2,1)S(1)} %all_to_all.5.codes, s32[1,32]{1,0:T(1,128)S(1)} %bitcast.2), custom_call_target="tpu_custom_call" | custom-call | tf_op jit(solution)/shard_map/fold/pallas_call | solution.py:449
  (1 shorter events, 0.0 us)
Async XLA Ops:
  0.0 1.6 %copy-start = (bf16[16,32,2048]{2,1,0:T(8,128)(2,1)S(1)}, bf16[16,32,2048]{2,1,0:T(8,128)(2,1)}, u32[]{:S(2)}) copy-start(bf16[16,32,2048]{2,1,0:T(8,128)(2,1)} %vol.5) | copy-start | bytes 6291460
  1.6 6.2 %copy-start.1 = (s32[32]{0:T(128)S(1)}, s32[32]{0:T(128)}, u32[]{:S(2)}) copy-start(s32[32]{0:T(128)} %param.3) | copy-start | bytes 388
  2.1 7.7 %collective-permute-start.1 = (bf16[17,16,2048]{2,1,0:T(8,128)(2,1)S(1)}, bf16[17,16,2048]{2,1,0:T(8,128)(2,1)S(1)}, u32[]{:S(2)}, u32[]{:S(2)}) collective-permute-start(bf16[17,16,2048]{2,1,0:T(8,128)(2,1)S(1)} %share.1), channel_id=1, source_target_pairs={{0,16},{16,0},{32,48},{48,32},{64,80},{80,64},{96,112},{112,96},{1... | collective-permute-start | bytes 3342344 | tf_op jit(solution)/shard_map/ppermute | solution.py:467
  4.7 7.6 %collective-permute-start = (bf16[32,2048]{1,0:T(8,128)(2,1)S(1)}, bf16[32,2048]{1,0:T(8,128)(2,1)S(1)}, u32[]{:S(2)}, u32[]{:S(2)}) collective-permute-start(bf16[32,2048]{1,0:T(8,128)(2,1)S(1)} %end.1), channel_id=1, source_target_pairs={{16,32},{48,64},{80,96},{112,128},{144,160},{176,192},{208,224},{2... | collective-permute-start | bytes 393224 | tf_op jit(solution)/shard_map/ppermute | solution.py:465
  10.1 7.5 %collective-permute-start.3 = (bf16[32,2048]{1,0:T(8,128)(2,1)S(1)}, bf16[32,2048]{1,0:T(8,128)(2,1)S(1)}, u32[]{:S(2)}, u32[]{:S(2)}) collective-permute-start(bf16[32,2048]{1,0:T(8,128)(2,1)S(1)} %rim_rows.1.rim), channel_id=1, source_target_pairs={{16,1},{1,16},{17,2},{2,17},{18,3},{3,18},{19,4},{4,19},{20,5},{5,... | collective-permute-start | bytes 393224 | tf_op jit(solution)/shard_map/ppermute | solution.py:477
  12.4 8.6 %collective-permute-start.2 = (bf16[16,2048]{1,0:T(8,128)(2,1)S(1)}, bf16[16,2048]{1,0:T(8,128)(2,1)S(1)}, u32[]{:S(2)}, u32[]{:S(2)}) collective-permute-start(bf16[16,2048]{1,0:T(8,128)(2,1)S(1)} %hand.1), channel_id=1, source_target_pairs={{0,16},{16,0},{32,48},{48,32},{64,80},{80,64},{96,112},{112,96},{1... | collective-permute-start | bytes 196616 | tf_op jit(solution)/shard_map/ppermute | solution.py:479

commit v7 on v6

--- a/solution.py
+++ b/solution.py
@@ -11,11 +11,12 @@
 F32 = jnp.float32
 BF16 = jnp.bfloat16
 LANES = 128
-TILES = 8
+TILES = 16
 LOG2E = 1.0 / math.log(2.0)
 FLOOR = -27.0
 STEPS = 2570.0
 TONE = 0.7 * 0.48 * 0.48
+FOOT = 0.4
 
 
 def recip(x):
@@ -35,6 +36,10 @@
     code = code.astype(jnp.int32)
     value = jnp.exp2(code.astype(F32) * (1.0 / STEPS) + (32768.0 / STEPS + FLOOR))
     return jnp.where(code == -32768, 0.0, value)
+
+
+def lower(stored):
+    return stored.astype(F32) - FOOT
 
 
 def core_index():
@@ -54,28 +59,17 @@
     return jnp.concatenate([ref[l, :, here].astype(F32)[row : row + 1] for l in range(16)], 0).astype(BF16)
 
 
-def end_kernel(vol, end):
-    depth = vol.shape[2]
-    layer = (vol.shape[0] - 1) * core_index()
-
-    def tile(z, carry):
-        here = lane_tile(LANES * z)
-        end[:, here] = vol[layer, :, here]
-        return carry
-
-    lax.fori_loop(0, depth // LANES, tile, 0, unroll=8)
-
-
-def share_kernel(vol, end, send):
+def share_kernel(vol, send, end):
     layers, rows, depth = vol.shape
     half = rows // 2
 
-    def share(far, row):
+    def share(far, row, face):
         def tile(z, carry):
             here = lane_tile(LANES * z)
             for l in range(layers):
                 send[l, :, here] = vol[l, pl.ds(far, half), here]
             send[layers, :, here] = one_row(vol, row, here)
+            end[:, here] = vol[face, :, here]
             return carry
 
         lax.fori_loop(0, depth // LANES, tile, 0, unroll=2)
@@ -84,11 +78,11 @@
 
     @pl.when(core == 0)
     def _():
-        share(half, half - 1)
-
-    @pl.when(core == 1)
-    def _():
-        share(0, half)
+        share(half, half - 1, 0)
+
+    @pl.when(core == 1)
+    def _():
+        share(0, half, layers - 1)
 
 
 def own_edge(vol, core, rim):
@@ -189,15 +183,15 @@
             square = gx * gx + gy * gy + gz * gz
             facing = gx + (0.6 / 0.48) * gy + (0.64 / 0.48) * gz
             shading = 0.3 / TONE + facing * facing * recip(square + 4.0)
-            lifted = jnp.maximum(v, 0.4)
-            density = jnp.minimum(lifted, 1.6) - 0.4
+            lifted = jnp.maximum(v, 0.0)
+            density = jnp.minimum(lifted, 1.2)
             path[t] = path[t] + density * (rate[0][...] - rate[1][...] * recip(square + 1.0))
             next_reach = jnp.exp2(path[t])
             weight = (next_reach - reach[t]) * shading
             reach[t] = next_reach
-            color[0][t] = color[0][t] + weight * jnp.clip(v, 0.8, 1.8)
-            color[1][t] = color[1][t] + weight * jnp.minimum(v, 2.0 - v)
-            color[2][t] = color[2][t] + weight * jnp.minimum(lifted, 1.2)
+            color[0][t] = color[0][t] + weight * jnp.clip(v, 0.8 - FOOT, 1.8 - FOOT)
+            color[1][t] = color[1][t] + weight * jnp.minimum(v, 2.0 - 2.0 * FOOT - v)
+            color[2][t] = color[2][t] + weight * jnp.minimum(lifted, 1.2 - FOOT)
             color[3][t] = color[3][t] + weight
 
     def keep(self, state, part):
@@ -229,12 +223,12 @@
 
     def widen(first, beside):
         def one(l, carry):
-            field[mine + l, 0] = jnp.zeros((rows, LANES), F32)
-            field[mine + l, tiles + 1] = jnp.zeros((rows, LANES), F32)
+            field[mine + l, 0] = jnp.full((rows, LANES), -FOOT, F32)
+            field[mine + l, tiles + 1] = jnp.full((rows, LANES), -FOOT, F32)
             for tile in range(tiles):
                 here = pl.ds(LANES * tile, LANES)
-                field[mine + l, tile + 1, pl.ds(8, half), :] = vol[l, pl.ds(first, half), here].astype(F32)
-                near = vol[l, pl.ds(half - first, half), here].astype(F32)
+                field[mine + l, tile + 1, pl.ds(8, half), :] = lower(vol[l, pl.ds(first, half), here])
+                near = lower(vol[l, pl.ds(half - first, half), here])
                 field[mine + l, tile + 1, pl.ds(beside[1], 8), :] = near[beside[0] : beside[0] + 8]
             return carry
 
@@ -269,17 +263,17 @@
     other = layers * (1 - core)
 
     def widen(l, carry):
-        field[other + l, 0, inside, :] = jnp.zeros((half, LANES), F32)
-        field[other + l, tiles + 1, inside, :] = jnp.zeros((half, LANES), F32)
+        field[other + l, 0, inside, :] = jnp.full((half, LANES), -FOOT, F32)
+        field[other + l, tiles + 1, inside, :] = jnp.full((half, LANES), -FOOT, F32)
         for tile in range(tiles):
-            field[other + l, tile + 1, inside, :] = mate[l, :, pl.ds(LANES * tile, LANES)].astype(F32)
+            field[other + l, tile + 1, inside, :] = lower(mate[l, :, pl.ds(LANES * tile, LANES)])
         return carry
 
     lax.fori_loop(0, layers, widen, 0)
 
     def border(slot, other):
         def tile(z, carry):
-            field[pl.ds(other, layers), z + 1, slot, :] = mate[layers, :, lane_tile(LANES * z)].astype(F32)
+            field[pl.ds(other, layers), z + 1, slot, :] = lower(mate[layers, :, lane_tile(LANES * z)])
             return carry
 
         lax.fori_loop(0, tiles, tile, 0, unroll=2)
@@ -314,7 +308,7 @@
 def rim_kernel(beyond, rates, field, part, beyond_wide):
     layers = field.shape[0]
     tiles = part.shape[2] // LANES
-    beyond_wide[...] = beyond[...].astype(F32)
+    beyond_wide[...] = lower(beyond[...])
     core = core_index()
     above, below = rim_masks(core)
     row = pl.multiple_of(8 + 8 * core, 8)
@@ -333,19 +327,19 @@
 def outer_kernel(face, handed, beyond, rates, own, other, border, field, codes, before_wide, after_wide, beyond_wide, levels):
     layers = field.shape[0]
     tiles = own.shape[2] // LANES
-    beyond_wide[...] = beyond[...].astype(F32)
+    beyond_wide[...] = lower(beyond[...])
     core = core_index()
     half = before_wide.shape[0]
 
     @pl.when(core == 0)
     def _():
-        before_wide[...] = face[pl.ds(0, half)].astype(F32)
-        after_wide[...] = handed[...].astype(F32)
-
-    @pl.when(core == 1)
-    def _():
-        before_wide[...] = handed[...].astype(F32)
-        after_wide[...] = face[pl.ds(half, half)].astype(F32)
+        before_wide[...] = lower(face[pl.ds(0, half)])
+        after_wide[...] = lower(handed[...])
+
+    @pl.when(core == 1)
+    def _():
+        before_wide[...] = lower(handed[...])
+        after_wide[...] = lower(face[pl.ds(half, half)])
 
     above, below = rim_masks(core)
     own_first = jnp.zeros((8, LANES), jnp.int32) + core == 0
@@ -371,7 +365,7 @@
                 path = state["path"][t]
                 red, green, blue, total = (kind[t] for kind in state["color"])
                 factor = jnp.where(side > 0, jnp.exp2(-path), -1.0) * TONE
-                final = [(red - 0.8 * total) * factor, green * factor, (1.2 * total - blue) * factor, jnp.abs(path)]
+                final = [(red - (0.8 - FOOT) * total) * factor, (green + FOOT * total) * factor, ((1.2 - FOOT) * total - blue) * factor, jnp.abs(path)]
                 for k in range(4):
                     levels[k, t, pl.ds(place, 8), :] = encode(final[k])
 
@@ -461,9 +455,10 @@
     work = 40 * layers * half * depth
     face, part = shape((half, depth), BF16), shape((5, 8, depth), F32)
     brick = shape((2 * layers, depth // LANES + 2, half + 16, LANES), F32)
-    end = call(end_kernel, (volume,), shape((rows, depth), BF16), [], "end")
+    send, end = call(
+        share_kernel, (volume,), (shape((layers + 1, half, depth), BF16), shape((rows, depth), BF16)), [], "share"
+    )
     end_in = lax.ppermute(end, "bx", chips)
-    send = call(share_kernel, (volume, end), shape((layers + 1, half, depth), BF16), [], "share")
     mate = lax.ppermute(send, "bx", mates)
     own, field, rates, own_rim = call(
         functools.partial(own_kernel, layers * size_x),

time: 40.2 us -> 40.1 us (level)
    pallas_call x9 -> x8, Pallas kernels: 10.2 us -> 10.2 us  [call(): pl.pallas_call(kernel, out_shape=out_shape, in_specs=[in_vmem] * len(oper...]
  transfers between devices with their start and end apart: 4 -> 4, of which waited for: 1 -> 1; matrix products, arithmetic and copies ran while one was open for 0% -> 0% of each run, Pallas kernels for 19% -> 20%
where the time goes in v7:
time: 40.1 us; the launch traced here: 39.9 us
  blocking collectives  17 us (42%)
  Pallas kernels  10.2 us (25%)
  starting transfers between devices  9.79 us (24%)
  local copies, waits for them, and re-layouts  1.59 us (4%)
  waiting for transfers between devices  1.17 us (3%)
    all_to_all x1, blocking collectives, body(): codes = lax.all_to_all(codes, 'bx', split_axis=0, concat_axis=0, tiled=True)  17 us
    pallas_call x8, Pallas kernels, call(): pl.pallas_call(kernel, out_shape=out_shape, in_specs=[in_vmem] * len(oper...  10.2 us
    ppermute x1, starting transfers between devices, body(): end_in = lax.ppermute(end, 'bx', chips)  3.1 us
    ppermute x1, starting transfers between devices, body(): mate = lax.ppermute(send, 'bx', mates)  2.57 us
    ppermute x1, starting transfers between devices, body(): beyond = lax.ppermute(rim, ('bx', 'by'), across)  2.2 us
    ppermute x1, starting transfers between devices, body(): handed = lax.ppermute(hand_on, 'bx', mates)  1.92 us
    unnamed x4, local copies, waits for them, and re-layouts  1.59 us
    ppermute x1, waiting for transfers between devices, body(): beyond = lax.ppermute(rim, ('bx', 'by'), across)  1.16 us
  transfers between devices with their start and end apart: 4, of which 1 were waited for; matrix products, arithmetic and copies ran while one was open for 0% of the time, Pallas kernels for 20%

profile of v7, /device:TPU:225, one launch (start us, length us, event | category | flops | bytes accessed | tf_op | source)
XLA Modules:
  0.0 39.9 jit_solution(16454911307491903177)
XLA Ops:
  0.0 0.0 copy-start
  0.0 1.6 %copy-done = bf16[16,32,2048]{2,1,0:T(8,128)(2,1)S(1)} copy-done((bf16[16,32,2048]{2,1,0:T(8,128)(2,1)S(1)}, bf16[16,32,2048]{2,1,0:T(8,128)(2,1)}, u32[]{:S(2)}) %copy-start) | copy-done | bytes 2097176
  1.6 0.0 copy-start.1
  1.6 0.5 %share.1 = (bf16[17,16,2048]{2,1,0:T(8,128)(2,1)S(1)}, bf16[32,2048]{1,0:T(8,128)(2,1)S(1)}) custom-call(bf16[16,32,2048]{2,1,0:T(8,128)(2,1)S(1)} %copy-done), custom_call_target="tpu_custom_call" | custom-call | tf_op jit(solution)/shard_map/share/pallas_call | solution.py:443
  2.1 2.6 %collective-permute-start.1 = (bf16[17,16,2048]{2,1,0:T(8,128)(2,1)S(1)}, bf16[17,16,2048]{2,1,0:T(8,128)(2,1)S(1)}, u32[]{:S(2)}, u32[]{:S(2)}) collective-permute-start(bf16[17,16,2048]{2,1,0:T(8,128)(2,1)S(1)} %get-tuple-element.14), channel_id=1, source_target_pairs={{0,16},{16,0},{32,48},{48,32},{64,80},{80,64},{96,112},{112,96},{1... | collective-permute-start | bytes 3342344 | tf_op jit(solution)/shard_map/ppermute | solution.py:462
  4.6 3.1 %collective-permute-start = (bf16[32,2048]{1,0:T(8,128)(2,1)S(1)}, bf16[32,2048]{1,0:T(8,128)(2,1)S(1)}, u32[]{:S(2)}, u32[]{:S(2)}) collective-permute-start(bf16[32,2048]{1,0:T(8,128)(2,1)S(1)} %get-tuple-element.13), channel_id=1, source_target_pairs={{16,32},{48,64},{80,96},{112,128},{144,160},{176,192},{208,224},{2... | collective-permute-start | bytes 393224 | tf_op jit(solution)/shard_map/ppermute | solution.py:461
  7.8 0.0 copy-done.1
  7.8 2.1 %own.1 = (f32[5,8,2048]{2,1,0:T(8,128)S(1)}, f32[32,18,32,128]{3,2,1,0:T(8,128)S(1)}, f32[2,32,128]{2,1,0:T(8,128)S(1)}, bf16[16,2048]{1,0:T(8,128)(2,1)S(1)}) custom-call(bf16[16,32,2048]{2,1,0:T(8,128)(2,1)S(1)} %copy-done, s32[1,32]{1,0:T(1,128)S(1)} %bitcast.1), custom_call_target="tpu_custom_call" | custom-call | flops 10485760 | bytes 2097152 | tf_op jit(solution)/shard_map/own/pallas_call | solution.py:443
  9.8 0.0 collective-permute-done.1.mate
  9.8 0.2 rim_rows.1.rim
  10.0 2.2 %collective-permute-start.3 = (bf16[32,2048]{1,0:T(8,128)(2,1)S(1)}, bf16[32,2048]{1,0:T(8,128)(2,1)S(1)}, u32[]{:S(2)}, u32[]{:S(2)}) collective-permute-start(bf16[32,2048]{1,0:T(8,128)(2,1)S(1)} %rim_rows.1.rim), channel_id=1, source_target_pairs={{16,1},{1,16},{17,2},{2,17},{18,3},{3,18},{19,4},{4,19},{20,5},{5,... | collective-permute-start | bytes 393224 | tf_op jit(solution)/shard_map/ppermute | solution.py:472
  12.3 0.0 collective-permute-done.face
  12.3 0.1 hand.1
  12.3 1.9 %collective-permute-start.2 = (bf16[16,2048]{1,0:T(8,128)(2,1)S(1)}, bf16[16,2048]{1,0:T(8,128)(2,1)S(1)}, u32[]{:S(2)}, u32[]{:S(2)}) collective-permute-start(bf16[16,2048]{1,0:T(8,128)(2,1)S(1)} %hand.1), channel_id=1, source_target_pairs={{0,16},{16,0},{32,48},{48,32},{64,80},{80,64},{96,112},{112,96},{1... | collective-permute-start | bytes 196616 | tf_op jit(solution)/shard_map/ppermute | solution.py:474
  14.3 2.1 %mate.1 = (f32[5,8,2048]{2,1,0:T(8,128)S(1)}, f32[32,18,32,128]{3,2,1,0:T(8,128)S(1)}) custom-call(bf16[17,16,2048]{2,1,0:T(8,128)(2,1)S(1)} %collective-permute-done.1.mate, f32[2,32,128]{2,1,0:T(8,128)S(1)} %get-tuple-element.16.rates, f32[32,18,32,128]{3,2,1,0:T(8,128)S(1)} %get-tuple-element.18.own_field), custom_call_target="tpu_custom_call", output_to_operand_aliasing={{1}: (2, {})} | custom-call | flops 10485760 | bytes 2097152 | tf_op jit(solution)/shard_map/mate/pallas_call | solution.py:443
  16.4 1.2 %collective-permute-done.3.beyond = bf16[32,2048]{1,0:T(8,128)(2,1)S(1)} collective-permute-done((bf16[32,2048]{1,0:T(8,128)(2,1)S(1)}, bf16[32,2048]{1,0:T(8,128)(2,1)S(1)}, u32[]{:S(2)}, u32[]{:S(2)}) %collective-permute-start.3) | collective-permute-done | bytes 131104 | tf_op jit(solution)/shard_map/ppermute | solution.py:472
  17.5 3.4 %rim.1.border = f32[5,8,2048]{2,1,0:T(8,128)S(1)} custom-call(bf16[32,2048]{1,0:T(8,128)(2,1)S(1)} %collective-permute-done.3.beyond, f32[2,32,128]{2,1,0:T(8,128)S(1)} %get-tuple-element.16.rates, f32[32,18,32,128]{3,2,1,0:T(8,128)S(1)} %get-tuple-element.20.field), custom_call_target="tpu_custom_call" | custom-call | flops 20971520 | bytes 2097152 | tf_op jit(solution)/shard_map/rim/pallas_call | solution.py:443
  20.9 0.0 collective-permute-done.2.handed
  20.9 1.0 %outer.1 = s16[32,2,16,128]{3,2,1,0:T(8,128)(2,1)S(1)} custom-call(bf16[32,2048]{1,0:T(8,128)(2,1)S(1)} %collective-permute-done.face, bf16[16,2048]{1,0:T(8,128)(2,1)S(1)} %collective-permute-done.2.handed, bf16[32,2048]{1,0:T(8,128)(2,1)S(1)} %collective-permute-done.3.beyond, f32[2,32,128]{2,1,0:T(8,128)S(1)} %get-tuple-element.16.rates, ...), custom_call_target="tpu_custom_call" | custom-call | flops 20971520 | bytes 2097152 | tf_op jit(solution)/shard_map/outer/pallas_call | solution.py:443
  21.9 17.0 %all_to_all.5.codes = s16[32,2,16,128]{3,2,1,0:T(8,128)(2,1)S(1)} all-to-all(s16[32,2,16,128]{3,2,1,0:T(8,128)(2,1)S(1)} %outer.1), channel_id=1, replica_groups=mesh['bx'=32,'by'=16] {'bx'}, dimensions={0} | all-to-all | bytes 524288 | tf_op jit(solution)/shard_map/all_to_all | solution.py:486
  39.0 0.9 %fold.1 = f32[4,32,64]{2,1,0:T(8,128)} custom-call(s16[32,2,16,128]{3,2,1,0:T(8,128)(2,1)S(1)} %all_to_all.5.codes, s32[1,32]{1,0:T(1,128)S(1)} %bitcast.2), custom_call_target="tpu_custom_call" | custom-call | tf_op jit(solution)/shard_map/fold/pallas_call | solution.py:443
Async XLA Ops:
  0.0 1.6 %copy-start = (bf16[16,32,2048]{2,1,0:T(8,128)(2,1)S(1)}, bf16[16,32,2048]{2,1,0:T(8,128)(2,1)}, u32[]{:S(2)}) copy-start(bf16[16,32,2048]{2,1,0:T(8,128)(2,1)} %vol.3) | copy-start | bytes 6291460
  1.6 6.2 %copy-start.1 = (s32[32]{0:T(128)S(1)}, s32[32]{0:T(128)}, u32[]{:S(2)}) copy-start(s32[32]{0:T(128)} %param.3) | copy-start | bytes 388
  2.1 7.8 %collective-permute-start.1 = (bf16[17,16,2048]{2,1,0:T(8,128)(2,1)S(1)}, bf16[17,16,2048]{2,1,0:T(8,128)(2,1)S(1)}, u32[]{:S(2)}, u32[]{:S(2)}) collective-permute-start(bf16[17,16,2048]{2,1,0:T(8,128)(2,1)S(1)} %get-tuple-element.14), channel_id=1, source_target_pairs={{0,16},{16,0},{32,48},{48,32},{64,80},{80,64},{96,112},{112,96},{1... | collective-permute-start | bytes 3342344 | tf_op jit(solution)/shard_map/ppermute | solution.py:462
  4.6 7.6 %collective-permute-start = (bf16[32,2048]{1,0:T(8,128)(2,1)S(1)}, bf16[32,2048]{1,0:T(8,128)(2,1)S(1)}, u32[]{:S(2)}, u32[]{:S(2)}) collective-permute-start(bf16[32,2048]{1,0:T(8,128)(2,1)S(1)} %get-tuple-element.13), channel_id=1, source_target_pairs={{16,32},{48,64},{80,96},{112,128},{144,160},{176,192},{208,224},{2... | collective-permute-start | bytes 393224 | tf_op jit(solution)/shard_map/ppermute | solution.py:461
  10.0 7.5 %collective-permute-start.3 = (bf16[32,2048]{1,0:T(8,128)(2,1)S(1)}, bf16[32,2048]{1,0:T(8,128)(2,1)S(1)}, u32[]{:S(2)}, u32[]{:S(2)}) collective-permute-start(bf16[32,2048]{1,0:T(8,128)(2,1)S(1)} %rim_rows.1.rim), channel_id=1, source_target_pairs={{16,1},{1,16},{17,2},{2,17},{18,3},{3,18},{19,4},{4,19},{20,5},{5,... | collective-permute-start | bytes 393224 | tf_op jit(solution)/shard_map/ppermute | solution.py:472
  12.3 8.6 %collective-permute-start.2 = (bf16[16,2048]{1,0:T(8,128)(2,1)S(1)}, bf16[16,2048]{1,0:T(8,128)(2,1)S(1)}, u32[]{:S(2)}, u32[]{:S(2)}) collective-permute-start(bf16[16,2048]{1,0:T(8,128)(2,1)S(1)} %hand.1), channel_id=1, source_target_pairs={{0,16},{16,0},{32,48},{48,32},{64,80},{80,64},{96,112},{112,96},{1... | collective-permute-start | bytes 196616 | tf_op jit(solution)/shard_map/ppermute | solution.py:474
